TPU v7x, 128 devices: a whole 4x4x4 slice. The times are simulated.
128 devices in a mesh: cfg: 2 (over z_hi), blk: 16 (over z_lo, x, core), ulysses: 4 (over y).
Axes of the slice: x: 4, y: 4, z: 4 (z_hi: 2, z_lo: 2; z = z_hi * 2 + z_lo), core: 2. Of those that a mesh axis runs over, the one named last changes fastest.
Arguments:
- latents: bfloat16 [8192, 3072], P(('blk', 'ulysses')), may hold values from -6 to 6
- w_qkv: bfloat16 [3072, 3, 3072], P(None, None, 'ulysses'), may hold values from -0.109375 to 0.109375
- w_out: bfloat16 [3072, 3072], P('ulysses'), may hold values from -0.109375 to 0.109375
- q_gain: float32 [128], replicated, may hold values from 1 to 3
- k_gain: float32 [128], replicated, may hold values from 1 to 3
- text_kv: bfloat16 [2, 2, 256, 3072], P(None, None, None, 'ulysses'), may hold values from -1000 to 1000, as said below
- text_lengths: int32 [2], replicated, may hold values from 64 to 256
- sigmas: float32 [51], replicated, may hold values from 0.02 to 1
- step_index: int32 [1], replicated, may hold values from 0 to 49
- guidance: float32 [1], replicated, may hold values from 4 to 8
Outputs:
- guided_velocity: bfloat16 [8192, 3072], P(('blk', 'ulysses'), 'cfg')
- next_latents: bfloat16 [8192, 3072], P(('blk', 'ulysses'), 'cfg')
Inputs may be any that keep to these rules, and one draw needn't show every extreme that they name: `text_kv`: text keys and values of both prompts.
All inputs are finite; a program needn't handle non-finite values.
Results may differ from a plain program's by a relative error of at most 0.019.
Values may be sent and summed in bfloat16 or wider, within the bound.
A program may use at most 128 MiB of HBM per device.

v0:
```python
import math

import jax
import jax.numpy as jnp
from jax import lax
from jax.sharding import PartitionSpec as P

HD = 128


epsilon = 1e-06
block_limit = 512


def partner(array, axis, distance):
    return lax.ppermute(array, axis, [(i, i ^ 1 << distance) for i in range(lax.axis_size(axis))])


def head_norm(values, gain_vector):
    shaped = values.reshape(values.shape[0], -1, HD)
    mean_square = jnp.mean(shaped * shaped, axis=-1, keepdims=True)
    return (shaped * lax.rsqrt(mean_square + epsilon) * gain_vector).astype(jnp.bfloat16)


def text_state(queries, text_keys, text_values, length_now, scale_factor):
    head_count = queries.shape[1]
    keys_shaped = text_keys.reshape(text_keys.shape[0], head_count, HD)
    values_shaped = text_values.reshape(text_values.shape[0], head_count, HD)
    scores = (
        jnp.einsum("qhd,khd->hqk", queries, keys_shaped, preferred_element_type=jnp.float32)
        * scale_factor
    )
    text_valid = jnp.arange(text_keys.shape[0])[None, None, :] < length_now
    scores = jnp.where(text_valid, scores, -jnp.inf)
    running_max = jnp.max(scores, axis=2)
    weights = jnp.exp(scores - running_max[:, :, None])
    weight_sum = jnp.sum(weights, axis=2)
    accumulated = jnp.einsum(
        "hqk,khd->qhd",
        weights.astype(jnp.bfloat16),
        values_shaped,
        preferred_element_type=jnp.float32,
    )
    return (running_max, weight_sum, accumulated)


def add_keys(carried_state, queries, key_block, value_block, scale_factor):
    running_max, weight_sum, accumulated = carried_state
    head_count = queries.shape[1]
    keys_shaped = key_block.reshape(key_block.shape[0], head_count, HD)
    values_shaped = value_block.reshape(value_block.shape[0], head_count, HD)
    scores = (
        jnp.einsum("qhd,khd->hqk", queries, keys_shaped, preferred_element_type=jnp.float32)
        * scale_factor
    )
    new_max = jnp.maximum(running_max, jnp.max(scores, axis=2))
    correction = jnp.exp(running_max - new_max)
    weights = jnp.exp(scores - new_max[:, :, None])
    weight_sum = weight_sum * correction + jnp.sum(weights, axis=2)
    accumulated = accumulated * correction.T[:, :, None] + jnp.einsum(
        "hqk,khd->qhd",
        weights.astype(jnp.bfloat16),
        values_shaped,
        preferred_element_type=jnp.float32,
    )
    return (new_max, weight_sum, accumulated)


def fold_keys(queries, scale_factor, carried_state, shard_piece):
    key_piece, value_piece = shard_piece
    piece_rows = key_piece.shape[0]
    key_blocks = key_piece.reshape(piece_rows // block_limit, block_limit, key_piece.shape[1])
    value_blocks = value_piece.reshape(piece_rows // block_limit, block_limit, value_piece.shape[1])

    def scan_step(carried, block_pair):
        return (add_keys(carried, queries, block_pair[0], block_pair[1], scale_factor), None)

    final_state, unused = lax.scan(scan_step, carried_state, (key_blocks, value_blocks))
    return final_state


def finish(carried_state):
    running_max, weight_sum, accumulated = carried_state
    normalized = accumulated / weight_sum.T[:, :, None]
    return normalized.reshape(normalized.shape[0], -1).astype(jnp.bfloat16)


def velocity_pair(attention, w_out, is_first):
    own_velocity = lax.optimization_barrier(
        lax.psum_scatter(
            jnp.dot(attention, w_out, preferred_element_type=jnp.float32).astype(jnp.bfloat16),
            "ulysses",
            scatter_dimension=0,
            tiled=True,
        )
    )
    other_velocity = partner(own_velocity, "cfg", 0)
    cond_velocity = jnp.where(is_first, own_velocity, other_velocity).astype(jnp.float32)
    uncond_velocity = jnp.where(is_first, other_velocity, own_velocity).astype(jnp.float32)
    return (cond_velocity, uncond_velocity)


def per_device(
    latents, w_qkv, w_out, q_gain, k_gain, text_kv, text_lengths, sigmas, step_index, guidance
):
    scale_factor = 1.0 / math.sqrt(HD)
    half_index = lax.axis_index("cfg")
    is_first = half_index == 0
    latent_now = latents
    projected = jnp.einsum(
        "rd,dce->rce",
        lax.all_gather(latent_now, "ulysses", axis=0, tiled=True),
        w_qkv,
        preferred_element_type=jnp.float32,
    )
    group_rows = projected.shape[0]
    queries = head_norm(projected[:, 0], q_gain)
    keys_here = head_norm(projected[:, 1], k_gain)
    values_here = projected[:, 2].astype(jnp.bfloat16)
    own_text = lax.dynamic_index_in_dim(text_kv, half_index, 0, keepdims=False)
    own_length = lax.dynamic_index_in_dim(text_lengths, half_index, 0, keepdims=False)
    start_state = text_state(queries, own_text[0], own_text[1], own_length, scale_factor)
    key_flat = keys_here.reshape(group_rows, -1)
    cycle_state = fold_keys(
        queries,
        scale_factor,
        start_state,
        (
            lax.all_gather(key_flat, "blk", axis=0, tiled=True),
            lax.all_gather(values_here, "blk", axis=0, tiled=True),
        ),
    )
    attention = finish(cycle_state)
    cond_velocity, uncond_velocity = velocity_pair(attention, w_out, is_first)
    guided = uncond_velocity + guidance[0] * (cond_velocity - uncond_velocity)
    position = step_index[0]
    sigma_step = sigmas[position + 1] - sigmas[position]
    latent_now = (latent_now.astype(jnp.float32) + sigma_step * guided).astype(jnp.bfloat16)
    column_count = latents.shape[1] // 2
    column_start = half_index * column_count
    guided_columns = lax.dynamic_slice_in_dim(guided, column_start, column_count, 1).astype(
        jnp.bfloat16
    )
    latent_columns = lax.dynamic_slice_in_dim(latent_now, column_start, column_count, 1)
    return (guided_columns, latent_columns)


def solution(mesh):
    placed = (
        P(("blk", "ulysses"), None),
        P(None, None, "ulysses"),
        P("ulysses", None),
        P(),
        P(),
        P(None, None, None, "ulysses"),
        P(),
        P(),
        P(),
        P(),
    )
    return jax.shard_map(
        per_device,
        mesh=mesh,
        in_specs=placed,
        out_specs=(P(("blk", "ulysses"), "cfg"), P(("blk", "ulysses"), "cfg")),
        check_vma=False,
    )
```

profile of v0, /device:TPU:1, one launch (start us, length us, event | category | flops | bytes accessed | tf_op | source)
XLA Modules:
  0.0 554.0 jit_solution(16518246786675820734)
XLA Ops:
  8.0 44.5 %all-gather.5.cloned.1.call-done = bf16[512,3072]{1,0:T(8,128)(2,1)} async-done(((bf16[128,3072]{1,0:T(8,128)(2,1)}), bf16[512,3072]{1,0:T(8,128)(2,1)}) %all-gather.5.cloned.1.call-update) | async-done | bytes 3145744 | tf_op jit(solution)/shard_map/all_gather | solution.py:112
  52.5 11.3 %fusion.11 = f32[512,3,768]{2,0,1:T(8,128)S(1)} fusion(bf16[3072,3,768]{2,0,1:T(8,128)(2,1)} %param.13, bf16[512,3072]{1,0:T(8,128)(2,1)} %all-gather.5.cloned.1.call-done), kind=kOutput, calls=%fused_computation.16 | convolution fusion | flops 7247757312 | bytes 22020096 | tf_op jit(solution)/shard_map/rd,dce->rce/dot_general | solution.py:110
  83.6 60.3 %all-gather.7.cloned.1.call-done = bf16[8192,768]{1,0:T(8,128)(2,1)} async-done(((bf16[512,768]{1,0:T(8,128)(2,1)}), bf16[8192,768]{1,0:T(8,128)(2,1)}) %all-gather.7.cloned.1.call-update) | async-done | bytes 12582928 | tf_op jit(solution)/shard_map/all_gather | solution.py:129
  143.9 74.4 %all-gather.9.cloned.1.call-done = bf16[8192,1,768]{2,0,1:T(8,128)(2,1)} async-done(((bf16[512,1,768]{2,0,1:T(8,128)(2,1)}), bf16[8192,1,768]{2,0,1:T(8,128)(2,1)}) %all-gather.9.cloned.1.call-update) | async-done | bytes 12582928 | tf_op jit(solution)/shard_map/all_gather | solution.py:130
  218.3 258.9 %while.14 = (s32[]{:T(128)}, f32[6,512]{1,0:T(8,128)S(1)}, f32[6,512]{1,0:T(8,128)S(1)}, f32[512,6,128]{0,2,1:T(8,128)}, bf16[16,512,768]{2,1,0:T(8,128)(2,1)}, ...) while((s32[]{:T(128)}, f32[6,512]{1,0:T(8,128)S(1)}, f32[6,512]{1,0:T(8,128)S(1)}, ...), condition=%wide.region_7.8_spmd, body=%wide.region_4.7_spmd.sunk | while | flops 818684928 | bytes 49741960 | solution.py:78
  221.0 4.9 bitcast_reduce_fusion.2
  227.4 6.0 %bitcast_add_fusion.2 = f32[512,6,128]{0,2,1:T(8,128)} fusion(f32[512,6,128]{0,2,1:T(8,128)} %get-tuple-element.150, bf16[512,6,128]{0,2,1:T(8,128)(2,1)S(1)} %bitcast.81, f32[6,512,512]{2,1,0:T(8,128)} %get-tuple-element.136, f32[6,512]{1,0:T(8,128)S(1)} %get-tuple-element.156, f32[512,6]{0,1:T(8,128)S(1)} %get-tuple-element.138), kind=kOutput, calls=%fused_computation.8.clone.1 | convolution fusion | flops 408158208 | bytes 10248192 | tf_op jit(solution)/shard_map/while/body/eval_jaxpr/hqk,khd->qhd/dot_general | solution.py:60
  237.2 4.9 bitcast_reduce_fusion.2
  243.6 6.0 %bitcast_add_fusion.2 = f32[512,6,128]{0,2,1:T(8,128)} fusion(f32[512,6,128]{0,2,1:T(8,128)} %get-tuple-element.150, bf16[512,6,128]{0,2,1:T(8,128)(2,1)S(1)} %bitcast.81, f32[6,512,512]{2,1,0:T(8,128)} %get-tuple-element.136, f32[6,512]{1,0:T(8,128)S(1)} %get-tuple-element.156, f32[512,6]{0,1:T(8,128)S(1)} %get-tuple-element.138), kind=kOutput, calls=%fused_computation.8.clone.1 | convolution fusion | flops 408158208 | bytes 10248192 | tf_op jit(solution)/shard_map/while/body/eval_jaxpr/hqk,khd->qhd/dot_general | solution.py:60
  253.4 4.9 bitcast_reduce_fusion.2
  259.8 6.0 %bitcast_add_fusion.2 = f32[512,6,128]{0,2,1:T(8,128)} fusion(f32[512,6,128]{0,2,1:T(8,128)} %get-tuple-element.150, bf16[512,6,128]{0,2,1:T(8,128)(2,1)S(1)} %bitcast.81, f32[6,512,512]{2,1,0:T(8,128)} %get-tuple-element.136, f32[6,512]{1,0:T(8,128)S(1)} %get-tuple-element.156, f32[512,6]{0,1:T(8,128)S(1)} %get-tuple-element.138), kind=kOutput, calls=%fused_computation.8.clone.1 | convolution fusion | flops 408158208 | bytes 10248192 | tf_op jit(solution)/shard_map/while/body/eval_jaxpr/hqk,khd->qhd/dot_general | solution.py:60
  269.6 4.9 bitcast_reduce_fusion.2
  276.0 6.0 %bitcast_add_fusion.2 = f32[512,6,128]{0,2,1:T(8,128)} fusion(f32[512,6,128]{0,2,1:T(8,128)} %get-tuple-element.150, bf16[512,6,128]{0,2,1:T(8,128)(2,1)S(1)} %bitcast.81, f32[6,512,512]{2,1,0:T(8,128)} %get-tuple-element.136, f32[6,512]{1,0:T(8,128)S(1)} %get-tuple-element.156, f32[512,6]{0,1:T(8,128)S(1)} %get-tuple-element.138), kind=kOutput, calls=%fused_computation.8.clone.1 | convolution fusion | flops 408158208 | bytes 10248192 | tf_op jit(solution)/shard_map/while/body/eval_jaxpr/hqk,khd->qhd/dot_general | solution.py:60
  285.7 4.9 bitcast_reduce_fusion.2
  292.2 6.0 %bitcast_add_fusion.2 = f32[512,6,128]{0,2,1:T(8,128)} fusion(f32[512,6,128]{0,2,1:T(8,128)} %get-tuple-element.150, bf16[512,6,128]{0,2,1:T(8,128)(2,1)S(1)} %bitcast.81, f32[6,512,512]{2,1,0:T(8,128)} %get-tuple-element.136, f32[6,512]{1,0:T(8,128)S(1)} %get-tuple-element.156, f32[512,6]{0,1:T(8,128)S(1)} %get-tuple-element.138), kind=kOutput, calls=%fused_computation.8.clone.1 | convolution fusion | flops 408158208 | bytes 10248192 | tf_op jit(solution)/shard_map/while/body/eval_jaxpr/hqk,khd->qhd/dot_general | solution.py:60
  301.9 4.9 bitcast_reduce_fusion.2
  308.4 6.0 %bitcast_add_fusion.2 = f32[512,6,128]{0,2,1:T(8,128)} fusion(f32[512,6,128]{0,2,1:T(8,128)} %get-tuple-element.150, bf16[512,6,128]{0,2,1:T(8,128)(2,1)S(1)} %bitcast.81, f32[6,512,512]{2,1,0:T(8,128)} %get-tuple-element.136, f32[6,512]{1,0:T(8,128)S(1)} %get-tuple-element.156, f32[512,6]{0,1:T(8,128)S(1)} %get-tuple-element.138), kind=kOutput, calls=%fused_computation.8.clone.1 | convolution fusion | flops 408158208 | bytes 10248192 | tf_op jit(solution)/shard_map/while/body/eval_jaxpr/hqk,khd->qhd/dot_general | solution.py:60
  324.6 6.0 %bitcast_add_fusion.2 = f32[512,6,128]{0,2,1:T(8,128)} fusion(f32[512,6,128]{0,2,1:T(8,128)} %get-tuple-element.150, bf16[512,6,128]{0,2,1:T(8,128)(2,1)S(1)} %bitcast.81, f32[6,512,512]{2,1,0:T(8,128)} %get-tuple-element.136, f32[6,512]{1,0:T(8,128)S(1)} %get-tuple-element.156, f32[512,6]{0,1:T(8,128)S(1)} %get-tuple-element.138), kind=kOutput, calls=%fused_computation.8.clone.1 | convolution fusion | flops 408158208 | bytes 10248192 | tf_op jit(solution)/shard_map/while/body/eval_jaxpr/hqk,khd->qhd/dot_general | solution.py:60
  334.3 4.9 bitcast_reduce_fusion.2
  340.7 6.0 %bitcast_add_fusion.2 = f32[512,6,128]{0,2,1:T(8,128)} fusion(f32[512,6,128]{0,2,1:T(8,128)} %get-tuple-element.150, bf16[512,6,128]{0,2,1:T(8,128)(2,1)S(1)} %bitcast.81, f32[6,512,512]{2,1,0:T(8,128)} %get-tuple-element.136, f32[6,512]{1,0:T(8,128)S(1)} %get-tuple-element.156, f32[512,6]{0,1:T(8,128)S(1)} %get-tuple-element.138), kind=kOutput, calls=%fused_computation.8.clone.1 | convolution fusion | flops 408158208 | bytes 10248192 | tf_op jit(solution)/shard_map/while/body/eval_jaxpr/hqk,khd->qhd/dot_general | solution.py:60
  350.5 4.9 bitcast_reduce_fusion.2
  356.9 6.0 %bitcast_add_fusion.2 = f32[512,6,128]{0,2,1:T(8,128)} fusion(f32[512,6,128]{0,2,1:T(8,128)} %get-tuple-element.150, bf16[512,6,128]{0,2,1:T(8,128)(2,1)S(1)} %bitcast.81, f32[6,512,512]{2,1,0:T(8,128)} %get-tuple-element.136, f32[6,512]{1,0:T(8,128)S(1)} %get-tuple-element.156, f32[512,6]{0,1:T(8,128)S(1)} %get-tuple-element.138), kind=kOutput, calls=%fused_computation.8.clone.1 | convolution fusion | flops 408158208 | bytes 10248192 | tf_op jit(solution)/shard_map/while/body/eval_jaxpr/hqk,khd->qhd/dot_general | solution.py:60
  373.1 6.0 %bitcast_add_fusion.2 = f32[512,6,128]{0,2,1:T(8,128)} fusion(f32[512,6,128]{0,2,1:T(8,128)} %get-tuple-element.150, bf16[512,6,128]{0,2,1:T(8,128)(2,1)S(1)} %bitcast.81, f32[6,512,512]{2,1,0:T(8,128)} %get-tuple-element.136, f32[6,512]{1,0:T(8,128)S(1)} %get-tuple-element.156, f32[512,6]{0,1:T(8,128)S(1)} %get-tuple-element.138), kind=kOutput, calls=%fused_computation.8.clone.1 | convolution fusion | flops 408158208 | bytes 10248192 | tf_op jit(solution)/shard_map/while/body/eval_jaxpr/hqk,khd->qhd/dot_general | solution.py:60
  389.3 6.0 %bitcast_add_fusion.2 = f32[512,6,128]{0,2,1:T(8,128)} fusion(f32[512,6,128]{0,2,1:T(8,128)} %get-tuple-element.150, bf16[512,6,128]{0,2,1:T(8,128)(2,1)S(1)} %bitcast.81, f32[6,512,512]{2,1,0:T(8,128)} %get-tuple-element.136, f32[6,512]{1,0:T(8,128)S(1)} %get-tuple-element.156, f32[512,6]{0,1:T(8,128)S(1)} %get-tuple-element.138), kind=kOutput, calls=%fused_computation.8.clone.1 | convolution fusion | flops 408158208 | bytes 10248192 | tf_op jit(solution)/shard_map/while/body/eval_jaxpr/hqk,khd->qhd/dot_general | solution.py:60
  405.5 6.0 %bitcast_add_fusion.2 = f32[512,6,128]{0,2,1:T(8,128)} fusion(f32[512,6,128]{0,2,1:T(8,128)} %get-tuple-element.150, bf16[512,6,128]{0,2,1:T(8,128)(2,1)S(1)} %bitcast.81, f32[6,512,512]{2,1,0:T(8,128)} %get-tuple-element.136, f32[6,512]{1,0:T(8,128)S(1)} %get-tuple-element.156, f32[512,6]{0,1:T(8,128)S(1)} %get-tuple-element.138), kind=kOutput, calls=%fused_computation.8.clone.1 | convolution fusion | flops 408158208 | bytes 10248192 | tf_op jit(solution)/shard_map/while/body/eval_jaxpr/hqk,khd->qhd/dot_general | solution.py:60
  421.7 6.0 %bitcast_add_fusion.2 = f32[512,6,128]{0,2,1:T(8,128)} fusion(f32[512,6,128]{0,2,1:T(8,128)} %get-tuple-element.150, bf16[512,6,128]{0,2,1:T(8,128)(2,1)S(1)} %bitcast.81, f32[6,512,512]{2,1,0:T(8,128)} %get-tuple-element.136, f32[6,512]{1,0:T(8,128)S(1)} %get-tuple-element.156, f32[512,6]{0,1:T(8,128)S(1)} %get-tuple-element.138), kind=kOutput, calls=%fused_computation.8.clone.1 | convolution fusion | flops 408158208 | bytes 10248192 | tf_op jit(solution)/shard_map/while/body/eval_jaxpr/hqk,khd->qhd/dot_general | solution.py:60
  437.9 6.0 %bitcast_add_fusion.2 = f32[512,6,128]{0,2,1:T(8,128)} fusion(f32[512,6,128]{0,2,1:T(8,128)} %get-tuple-element.150, bf16[512,6,128]{0,2,1:T(8,128)(2,1)S(1)} %bitcast.81, f32[6,512,512]{2,1,0:T(8,128)} %get-tuple-element.136, f32[6,512]{1,0:T(8,128)S(1)} %get-tuple-element.156, f32[512,6]{0,1:T(8,128)S(1)} %get-tuple-element.138), kind=kOutput, calls=%fused_computation.8.clone.1 | convolution fusion | flops 408158208 | bytes 10248192 | tf_op jit(solution)/shard_map/while/body/eval_jaxpr/hqk,khd->qhd/dot_general | solution.py:60
  454.0 6.0 %bitcast_add_fusion.2 = f32[512,6,128]{0,2,1:T(8,128)} fusion(f32[512,6,128]{0,2,1:T(8,128)} %get-tuple-element.150, bf16[512,6,128]{0,2,1:T(8,128)(2,1)S(1)} %bitcast.81, f32[6,512,512]{2,1,0:T(8,128)} %get-tuple-element.136, f32[6,512]{1,0:T(8,128)S(1)} %get-tuple-element.156, f32[512,6]{0,1:T(8,128)S(1)} %get-tuple-element.138), kind=kOutput, calls=%fused_computation.8.clone.1 | convolution fusion | flops 408158208 | bytes 10248192 | tf_op jit(solution)/shard_map/while/body/eval_jaxpr/hqk,khd->qhd/dot_general | solution.py:60
  470.2 6.0 %bitcast_add_fusion.2 = f32[512,6,128]{0,2,1:T(8,128)} fusion(f32[512,6,128]{0,2,1:T(8,128)} %get-tuple-element.150, bf16[512,6,128]{0,2,1:T(8,128)(2,1)S(1)} %bitcast.81, f32[6,512,512]{2,1,0:T(8,128)} %get-tuple-element.136, f32[6,512]{1,0:T(8,128)S(1)} %get-tuple-element.156, f32[512,6]{0,1:T(8,128)S(1)} %get-tuple-element.138), kind=kOutput, calls=%fused_computation.8.clone.1 | convolution fusion | flops 408158208 | bytes 10248192 | tf_op jit(solution)/shard_map/while/body/eval_jaxpr/hqk,khd->qhd/dot_general | solution.py:60
  478.9 6.4 %convolution_convert_fusion = bf16[512,3072]{1,0:T(8,128)(2,1)} fusion(bf16[512,768]{0,1:T(8,128)(2,1)S(1)} %bitcast.92, bf16[768,3072]{1,0:T(8,128)(2,1)} %param.14), kind=kOutput, calls=%fused_computation.15 | convolution fusion | flops 2417491968 | bytes 8650752 | tf_op jit(solution)/shard_map/dot_general | solution.py:91
  485.3 38.8 %reduce-scatter.2.cloned.1.call-done = bf16[128,3072]{1,0:T(8,128)(2,1)} async-done(((bf16[512,3072]{1,0:T(8,128)(2,1)}), bf16[128,3072]{1,0:T(8,128)(2,1)}) %reduce-scatter.2.cloned.1.call-update) | async-done | bytes 786448 | tf_op jit(solution)/shard_map/reduce_scatter | solution.py:90
  530.2 14.1 %collective-permute-done = bf16[128,3072]{1,0:T(8,128)(2,1)S(1)} collective-permute-done((bf16[128,3072]{1,0:T(8,128)(2,1)}, bf16[128,3072]{1,0:T(8,128)(2,1)S(1)}, u32[]{:S(2)}, u32[]{:S(2)}) %collective-permute-start) | collective-permute-done | bytes 786464 | tf_op jit(solution)/shard_map/ppermute | solution.py:16
  (254 shorter events, 152.5 us)
Async XLA Ops:
  7.2 45.3 %all-gather.5.cloned.1.call-start = ((), (), s32[]{:S(2)}) async-start(), calls=%async_computation.1 | async-start | bytes 3932160 | tf_op jit(solution)/shard_map/all_gather | solution.py:112
  7.9 136.0 %all-gather.7.cloned.1.call-start = ((), (), s32[]{:S(2)}) async-start(), calls=%async_computation.2 | async-start | bytes 13369344 | tf_op jit(solution)/shard_map/all_gather | solution.py:129
  71.2 6.4 %copy-start.3 = (f32[512,1,768]{2,0,1:T(8,128)S(1)}, f32[512,1,768]{2,0,1:T(8,128)}, u32[]{:S(2)}) copy-start(f32[512,1,768]{2,0,1:T(8,128)} %get-tuple-element.77) | copy-start | bytes 4718596
  71.2 147.1 %all-gather.9.cloned.1.call-start = ((), (), s32[]{:S(2)}) async-start(), calls=%async_computation.4 | async-start | bytes 13369344 | tf_op jit(solution)/shard_map/all_gather | solution.py:130
  73.8 450.3 %reduce-scatter.2.cloned.1.call-start = ((), (), s32[]{:S(2)}) async-start(), calls=%async_computation.3 | async-start | bytes 3932160 | tf_op jit(solution)/shard_map/reduce_scatter | solution.py:90
  225.9 7.5 %slice-start = ((s8[6291456]{0:T(1024)(128)(4,1)}), s8[2097152]{0:T(1024)(128)(4,1)S(1)}, s32[]{:S(2)}) async-start(s8[6291456]{0:T(1024)(128)(4,1)} %bitcast.79), calls=%async_computation.5 | async-start | bytes 4194304 | tf_op jit(solution)/shard_map/while
  242.1 7.5 %slice-start = ((s8[6291456]{0:T(1024)(128)(4,1)}), s8[2097152]{0:T(1024)(128)(4,1)S(1)}, s32[]{:S(2)}) async-start(s8[6291456]{0:T(1024)(128)(4,1)} %bitcast.79), calls=%async_computation.5 | async-start | bytes 4194304 | tf_op jit(solution)/shard_map/while
  243.6 6.0 %slice-start.1 = ((s8[6291456]{0:T(1024)(128)(4,1)}), s8[4194304]{0:T(1024)(128)(4,1)S(1)}, s32[]{:S(2)}) async-start(s8[6291456]{0:T(1024)(128)(4,1)} %bitcast.79), calls=%async_computation.6 | async-start | bytes 8388608 | tf_op jit(solution)/shard_map/while
  258.2 7.5 %slice-start = ((s8[6291456]{0:T(1024)(128)(4,1)}), s8[2097152]{0:T(1024)(128)(4,1)S(1)}, s32[]{:S(2)}) async-start(s8[6291456]{0:T(1024)(128)(4,1)} %bitcast.79), calls=%async_computation.5 | async-start | bytes 4194304 | tf_op jit(solution)/shard_map/while
  259.8 6.0 %slice-start.1 = ((s8[6291456]{0:T(1024)(128)(4,1)}), s8[4194304]{0:T(1024)(128)(4,1)S(1)}, s32[]{:S(2)}) async-start(s8[6291456]{0:T(1024)(128)(4,1)} %bitcast.79), calls=%async_computation.6 | async-start | bytes 8388608 | tf_op jit(solution)/shard_map/while
  274.4 7.5 %slice-start = ((s8[6291456]{0:T(1024)(128)(4,1)}), s8[2097152]{0:T(1024)(128)(4,1)S(1)}, s32[]{:S(2)}) async-start(s8[6291456]{0:T(1024)(128)(4,1)} %bitcast.79), calls=%async_computation.5 | async-start | bytes 4194304 | tf_op jit(solution)/shard_map/while
  276.0 6.0 %slice-start.1 = ((s8[6291456]{0:T(1024)(128)(4,1)}), s8[4194304]{0:T(1024)(128)(4,1)S(1)}, s32[]{:S(2)}) async-start(s8[6291456]{0:T(1024)(128)(4,1)} %bitcast.79), calls=%async_computation.6 | async-start | bytes 8388608 | tf_op jit(solution)/shard_map/while
  290.6 7.5 %slice-start = ((s8[6291456]{0:T(1024)(128)(4,1)}), s8[2097152]{0:T(1024)(128)(4,1)S(1)}, s32[]{:S(2)}) async-start(s8[6291456]{0:T(1024)(128)(4,1)} %bitcast.79), calls=%async_computation.5 | async-start | bytes 4194304 | tf_op jit(solution)/shard_map/while
  292.2 6.0 %slice-start.1 = ((s8[6291456]{0:T(1024)(128)(4,1)}), s8[4194304]{0:T(1024)(128)(4,1)S(1)}, s32[]{:S(2)}) async-start(s8[6291456]{0:T(1024)(128)(4,1)} %bitcast.79), calls=%async_computation.6 | async-start | bytes 8388608 | tf_op jit(solution)/shard_map/while
  306.8 7.5 %slice-start = ((s8[6291456]{0:T(1024)(128)(4,1)}), s8[2097152]{0:T(1024)(128)(4,1)S(1)}, s32[]{:S(2)}) async-start(s8[6291456]{0:T(1024)(128)(4,1)} %bitcast.79), calls=%async_computation.5 | async-start | bytes 4194304 | tf_op jit(solution)/shard_map/while
  323.0 7.5 %slice-start = ((s8[6291456]{0:T(1024)(128)(4,1)}), s8[2097152]{0:T(1024)(128)(4,1)S(1)}, s32[]{:S(2)}) async-start(s8[6291456]{0:T(1024)(128)(4,1)} %bitcast.79), calls=%async_computation.5 | async-start | bytes 4194304 | tf_op jit(solution)/shard_map/while
  324.5 6.0 %slice-start.1 = ((s8[6291456]{0:T(1024)(128)(4,1)}), s8[4194304]{0:T(1024)(128)(4,1)S(1)}, s32[]{:S(2)}) async-start(s8[6291456]{0:T(1024)(128)(4,1)} %bitcast.79), calls=%async_computation.6 | async-start | bytes 8388608 | tf_op jit(solution)/shard_map/while
  339.2 7.5 %slice-start = ((s8[6291456]{0:T(1024)(128)(4,1)}), s8[2097152]{0:T(1024)(128)(4,1)S(1)}, s32[]{:S(2)}) async-start(s8[6291456]{0:T(1024)(128)(4,1)} %bitcast.79), calls=%async_computation.5 | async-start | bytes 4194304 | tf_op jit(solution)/shard_map/while
  340.7 6.0 %slice-start.1 = ((s8[6291456]{0:T(1024)(128)(4,1)}), s8[4194304]{0:T(1024)(128)(4,1)S(1)}, s32[]{:S(2)}) async-start(s8[6291456]{0:T(1024)(128)(4,1)} %bitcast.79), calls=%async_computation.6 | async-start | bytes 8388608 | tf_op jit(solution)/shard_map/while
  355.3 7.5 %slice-start = ((s8[6291456]{0:T(1024)(128)(4,1)}), s8[2097152]{0:T(1024)(128)(4,1)S(1)}, s32[]{:S(2)}) async-start(s8[6291456]{0:T(1024)(128)(4,1)} %bitcast.79), calls=%async_computation.5 | async-start | bytes 4194304 | tf_op jit(solution)/shard_map/while
  371.5 7.5 %slice-start = ((s8[6291456]{0:T(1024)(128)(4,1)}), s8[2097152]{0:T(1024)(128)(4,1)S(1)}, s32[]{:S(2)}) async-start(s8[6291456]{0:T(1024)(128)(4,1)} %bitcast.79), calls=%async_computation.5 | async-start | bytes 4194304 | tf_op jit(solution)/shard_map/while
  387.7 7.5 %slice-start = ((s8[6291456]{0:T(1024)(128)(4,1)}), s8[2097152]{0:T(1024)(128)(4,1)S(1)}, s32[]{:S(2)}) async-start(s8[6291456]{0:T(1024)(128)(4,1)} %bitcast.79), calls=%async_computation.5 | async-start | bytes 4194304 | tf_op jit(solution)/shard_map/while
  403.9 7.5 %slice-start = ((s8[6291456]{0:T(1024)(128)(4,1)}), s8[2097152]{0:T(1024)(128)(4,1)S(1)}, s32[]{:S(2)}) async-start(s8[6291456]{0:T(1024)(128)(4,1)} %bitcast.79), calls=%async_computation.5 | async-start | bytes 4194304 | tf_op jit(solution)/shard_map/while
  420.1 7.5 %slice-start = ((s8[6291456]{0:T(1024)(128)(4,1)}), s8[2097152]{0:T(1024)(128)(4,1)S(1)}, s32[]{:S(2)}) async-start(s8[6291456]{0:T(1024)(128)(4,1)} %bitcast.79), calls=%async_computation.5 | async-start | bytes 4194304 | tf_op jit(solution)/shard_map/while
  436.3 7.5 %slice-start = ((s8[6291456]{0:T(1024)(128)(4,1)}), s8[2097152]{0:T(1024)(128)(4,1)S(1)}, s32[]{:S(2)}) async-start(s8[6291456]{0:T(1024)(128)(4,1)} %bitcast.79), calls=%async_computation.5 | async-start | bytes 4194304 | tf_op jit(solution)/shard_map/while
  437.8 6.0 %slice-start.1 = ((s8[6291456]{0:T(1024)(128)(4,1)}), s8[4194304]{0:T(1024)(128)(4,1)S(1)}, s32[]{:S(2)}) async-start(s8[6291456]{0:T(1024)(128)(4,1)} %bitcast.79), calls=%async_computation.6 | async-start | bytes 8388608 | tf_op jit(solution)/shard_map/while
  452.5 7.5 %slice-start = ((s8[6291456]{0:T(1024)(128)(4,1)}), s8[2097152]{0:T(1024)(128)(4,1)S(1)}, s32[]{:S(2)}) async-start(s8[6291456]{0:T(1024)(128)(4,1)} %bitcast.79), calls=%async_computation.5 | async-start | bytes 4194304 | tf_op jit(solution)/shard_map/while
  468.6 7.5 %slice-start = ((s8[6291456]{0:T(1024)(128)(4,1)}), s8[2097152]{0:T(1024)(128)(4,1)S(1)}, s32[]{:S(2)}) async-start(s8[6291456]{0:T(1024)(128)(4,1)} %bitcast.79), calls=%async_computation.5 | async-start | bytes 4194304 | tf_op jit(solution)/shard_map/while
  485.3 43.0 %copy-start.6 = (f32[51]{0:T(128)S(1)}, f32[51]{0:T(128)}, u32[]{:S(2)}) copy-start(f32[51]{0:T(128)} %param.19) | copy-start | bytes 616
  485.3 61.4 %copy-start.4 = (bf16[128,3072]{1,0:T(8,128)(2,1)S(1)}, bf16[128,3072]{1,0:T(8,128)(2,1)}, u32[]{:S(2)}) copy-start(bf16[128,3072]{1,0:T(8,128)(2,1)} %param.12) | copy-start | bytes 2359300
  485.3 62.2 %copy-start.1 = (f32[128]{0:T(128)S(1)}, f32[128]{0:T(128)}, u32[]{:S(2)}) copy-start(f32[128]{0:T(128)} %param.16) | copy-start | bytes 1540
  524.1 20.2 %collective-permute-start = (bf16[128,3072]{1,0:T(8,128)(2,1)}, bf16[128,3072]{1,0:T(8,128)(2,1)S(1)}, u32[]{:S(2)}, u32[]{:S(2)}) collective-permute-start(bf16[128,3072]{1,0:T(8,128)(2,1)} %reduce-scatter.2.cloned.1.call-done), channel_id=1, source_target_pairs={{0,64},{64,0},{1,65},{65,1},{2,66},{66,2},{3,67},{67,3},{4,68},{68... | collective-permute-start | bytes 2359304 | tf_op jit(solution)/shard_map/ppermute | solution.py:16
  (14 other events, 66.1 us)
Sparse Core Ops, SparseCore 0:
  9.7 42.7 all-gather.4
  71.4 72.4 all-gather.6
  145.6 72.6 all-gather.8
  485.4 38.6 reduce-scatter.1
where the time goes:
time: 556 us; the launch traced here: 554 us
  waiting for transfers between devices  233 us (42%)
  matrix products  193 us (35%)
  local copies, waits for them, and re-layouts  79.7 us (14%)
  other arithmetic  27.2 us (5%)
  between operations  16.6 us (3%)
    dot_general x16, matrix products, add_keys(): jnp.einsum('hqk,khd->qhd', weights.astype(jnp.bfloat16), values_shaped, p...  95.3 us
    dot_general x16, matrix products, add_keys(): jnp.einsum('qhd,khd->hqk', queries, keys_shaped, preferred_element_type=j...  77.6 us
    all_gather x1, waiting for transfers between devices, per_device(): lax.all_gather(values_here, 'blk', axis=0, tiled=True)  74.4 us
    dynamic_slice x48, local copies, waits for them, and re-layouts, fold_keys(): lax.scan(scan_step, carried_state, (key_blocks, value_blocks))  67.8 us
    all_gather x1, waiting for transfers between devices, per_device(): lax.all_gather(key_flat, 'blk', axis=0, tiled=True)  60.3 us
    all_gather x1, waiting for transfers between devices, per_device(): lax.all_gather(latent_now, 'ulysses', axis=0, tiled=True)  44.5 us
    reduce_scatter x1, waiting for transfers between devices, velocity_pair(): lax.psum_scatter(jnp.dot(attention, w_out, preferred_element_type=jnp.flo...  38.8 us
    reduce_sum x16, other arithmetic, add_keys(): weight_sum = weight_sum * correction + jnp.sum(weights, axis=2)  16.6 us
  transfers between devices with their start and end apart: 5, of which 5 were waited for; matrix products, arithmetic and copies ran while one was open for 2% of the time, Pallas kernels for 0%

commit v1 on v0

v1 whole, which is shorter than its diff:
```python
import functools
import math

import jax
import jax.numpy as jnp
from jax import lax
from jax.experimental import pallas as pl
from jax.experimental.pallas import tpu as pltpu
from jax.sharding import PartitionSpec as P

HD = 128
EPS = 1e-06
LOG2E = math.log2(math.e)
SCORE = LOG2E / math.sqrt(HD)
MESH = pl.DeviceIdType.MESH
NT = (((1,), (1,)), ((), ()))
TN = (((0,), (0,)), ((), ()))
F32 = jnp.float32
BF16 = jnp.bfloat16

HEADS = 3
ROWS = 64
GROUP = 8 * ROWS
WIDTH = 3072
HALF = WIDTH // 2
OWN = HEADS * HD
KEY_CHUNK = 256
OUT_CHUNK = 768
MESSAGES = 128


def place():
    blk = lax.axis_index("blk")
    z_hi = lax.axis_index("cfg")
    core = lax.rem(blk, 2)
    x = lax.rem(lax.div(blk, 2), 4)
    z = z_hi * 2 + lax.div(blk, 8)
    return x, lax.axis_index("ulysses"), z, core, z_hi


def step_kernel(
    x_hbm,
    wqkv_hbm,
    wout_hbm,
    text_hbm,
    qgain_ref,
    kgain_ref,
    lengths_ref,
    sigmas_ref,
    index_ref,
    guidance_ref,
    guided_ref,
    next_ref,
    xg,
    wq,
    wo,
    text,
    xcols,
    qbuf,
    kbuf,
    vbuf,
    qtext,
    textout,
    textstat,
    osend,
    orecv,
    lsend,
    lrecv,
    oown,
    lown,
    asend,
    abuf,
    dsend,
    drecv,
    nsend,
    nrecv,
    pown,
    csend,
    crecv,
    local_sem,
    send_sem,
    recv_sem,
):
    x, y, z, core, z_hi = place()

    def device(dx, dy, dz, dc):
        tx = lax.rem(x + dx + 4, 4)
        ty = lax.rem(y + dy + 4, 4)
        tz = lax.rem(z + dz + 4, 4)
        tc = lax.rem(core + dc, 2)
        return (lax.div(tz, 2), lax.rem(tz, 2) * 8 + tx * 2 + tc, ty)

    def key_device(d):
        return device((1 - core) * d, 0, core * d, 0)

    def query_device(d):
        return device(core * d, 0, (1 - core) * d, 0)

    locals_started = []

    def local(src, dst):
        copy = pltpu.make_async_copy(src, dst, local_sem.at[len(locals_started)])
        copy.start()
        locals_started.append(copy)
        return copy

    own_rows = x_hbm.at[pl.ds(pl.multiple_of(z_hi * ROWS, ROWS), ROWS)]
    own_copy = local(own_rows, xg.at[0, 0])
    own_col = core * OWN
    w_copies = []
    order = [(1, 0), (2, 0), (0, 0), (1, 1), (2, 1), (0, 1), (1, 2), (2, 2), (0, 2)]
    for place_at, (which, head) in enumerate(order):
        w_copies.append(
            local(
                wqkv_hbm.at[which, :, pl.ds(pl.multiple_of(own_col + head * HD, HD), HD)],
                wq.at[:, pl.ds(place_at * HD, HD)],
            )
        )
    text_copy = local(text_hbm.at[:, :, :, pl.ds(pl.multiple_of(own_col, HD), OWN)], text)
    wo_copies = []
    for rel_row in range(2):
        row_at = (core if rel_row == 0 else 1 - core) * OWN
        for rel_col in range(2):
            col_at = (1 - z_hi if rel_col == 0 else z_hi) * HALF
            wo_copies.append(
                local(
                    wout_hbm.at[
                        pl.ds(pl.multiple_of(row_at, OWN), OWN),
                        pl.ds(pl.multiple_of(col_at, HALF), HALF),
                    ],
                    wo.at[pl.ds(rel_row * OWN, OWN), pl.ds(rel_col * HALF, HALF)],
                )
            )
    xcols_copy = local(x_hbm.at[:, pl.ds(pl.multiple_of(z_hi * HALF, HALF), HALF)], xcols)

    barrier = pltpu.get_barrier_semaphore()
    greeted = [
        (0, 1, 0, 0),
        (0, -1, 0, 0),
        (0, 0, 0, 1),
        (1, 0, 0, 0),
        (-1, 0, 0, 0),
        (2, 0, 0, 0),
        (0, 0, 1, 0),
        (0, 0, -1, 0),
        (0, 0, 2, 0),
    ]
    for offset in greeted:
        pl.semaphore_signal(barrier, inc=1, device_id=device(*offset), device_id_type=MESH)
    pl.semaphore_wait(barrier, len(greeted))

    sent = []

    def send(src, dst, to):
        number = len(sent)
        copy = pltpu.make_async_remote_copy(
            src_ref=src,
            dst_ref=dst,
            send_sem=send_sem.at[number],
            recv_sem=recv_sem.at[number],
            device_id=to,
            device_id_type=MESH,
        )
        copy.start()
        sent.append(copy)
        return copy

    up, down, other = device(0, 1, 0, 0), device(0, -1, 0, 0), device(0, 0, 0, 1)
    low, high = pl.ds(0, ROWS // 2), pl.ds(ROWS // 2, ROWS // 2)

    def own_part(part):
        return x_hbm.at[pl.ds(pl.multiple_of(z_hi * ROWS + part * (ROWS // 2), ROWS // 2), ROWS // 2)]

    up_low = send(own_part(0), xg.at[0, 1, low], up)
    down_high = send(own_part(1), xg.at[0, 2, high], down)
    up_high = send(own_part(1), xg.at[0, 1, high], up)
    down_low = send(own_part(0), xg.at[0, 2, low], down)
    to_other = [send(own_rows, xg.at[1, 0], other)]
    up_low.wait_recv()
    far_low = send(xg.at[0, 1, low], xg.at[0, 3, low], up)
    down_high.wait_recv()
    far_high = send(xg.at[0, 2, high], xg.at[0, 3, high], down)
    up_high.wait_recv()
    to_other.append(send(xg.at[0, 1], xg.at[1, 1], other))
    down_low.wait_recv()
    to_other.append(send(xg.at[0, 2], xg.at[1, 2], other))
    own_copy.wait()
    for copy in w_copies:
        copy.wait()
    far_low.wait_recv()
    far_high.wait_recv()
    to_other.append(send(xg.at[0, 3], xg.at[1, 3], other))
    for copy in to_other:
        copy.wait_recv()

    def normed(value, gain):
        mean_square = jnp.mean(value * value, axis=1, keepdims=True)
        return value * lax.rsqrt(mean_square + EPS) * gain

    def keep(which, head, value):
        if which == 0:
            query = normed(value, qgain_ref[...])
            qtext[head] = query.astype(BF16)
            qbuf[head, 0] = (query * SCORE).astype(BF16)
        elif which == 1:
            kbuf[head, 0] = normed(value, kgain_ref[...]).astype(BF16)
        else:
            vbuf[head, 0] = value.T.astype(BF16)

    latents = xg[...].reshape(GROUP, WIDTH)
    near = {}

    def send_near(head):
        near[head] = [
            send(kbuf.at[head, 0], kbuf.at[head, 1], key_device(1)),
            send(vbuf.at[head, 0], vbuf.at[head, 1], key_device(1)),
            send(qbuf.at[head, 0], qbuf.at[head, 1], query_device(1)),
            send(kbuf.at[head, 0], kbuf.at[head, 2], key_device(-1)),
            send(vbuf.at[head, 0], vbuf.at[head, 2], key_device(-1)),
            send(qbuf.at[head, 0], qbuf.at[head, 2], query_device(-1)),
        ]

    done = 0
    for start in range(0, len(order), 2):
        pair = order[start : start + 2]
        product = jnp.dot(
            latents,
            wq[:, start * HD : (start + len(pair)) * HD],
            preferred_element_type=F32,
        )
        for i, (which, head) in enumerate(pair):
            keep(which, head, product[:, i * HD : (i + 1) * HD])
        while done < HEADS and start + len(pair) >= 3 * (done + 1):
            send_near(done)
            done += 1

    far = {}

    def send_far(head):
        for copy in near[head]:
            copy.wait_recv()
        a, b = pl.ds(0, GROUP // 2), pl.ds(GROUP // 2, GROUP // 2)
        va, vb = pl.ds(0, HD // 2), pl.ds(HD // 2, HD // 2)
        far[head] = [
            send(kbuf.at[head, 1, a], kbuf.at[head, 3, a], key_device(1)),
            send(vbuf.at[head, 1, va], vbuf.at[head, 3, va], key_device(1)),
            send(qbuf.at[head, 1, a], qbuf.at[head, 3, a], query_device(1)),
            send(kbuf.at[head, 2, b], kbuf.at[head, 3, b], key_device(-1)),
            send(vbuf.at[head, 2, vb], vbuf.at[head, 3, vb], key_device(-1)),
            send(qbuf.at[head, 2, b], qbuf.at[head, 3, b], query_device(-1)),
        ]

    text_copy.wait()

    def text_attention(head):
        columns = slice(head * HD, (head + 1) * HD)
        for half in range(2):
            scores = (
                lax.dot_general(text[half, 0, :, columns], qtext[head], NT, preferred_element_type=F32)
                * SCORE
            )
            valid = lax.broadcasted_iota(jnp.int32, scores.shape, 0) < lengths_ref[half]
            scores = jnp.where(valid, scores, -jnp.inf)
            top = jnp.max(scores, axis=0, keepdims=True)
            weights = jnp.exp2(scores - top)
            total = jnp.sum(weights, axis=0, keepdims=True)
            textout[head, half] = lax.dot_general(
                text[half, 1, :, columns], weights.astype(BF16), TN, preferred_element_type=F32
            )
            textstat[head, half, 0:1] = top
            textstat[head, half, 1:2] = total

    back = {}

    def attend(head):
        for copy in far[head]:
            copy.wait_recv()
        queries = qbuf[head].reshape(4 * GROUP, HD)
        top = total = weighted = None
        for slot in range(4):
            for at in range(0, GROUP, KEY_CHUNK):
                scores = lax.dot_general(
                    kbuf[head, slot, at : at + KEY_CHUNK], queries, NT, preferred_element_type=F32
                )
                chunk_top = jnp.max(scores, axis=0, keepdims=True)
                new_top = chunk_top if top is None else jnp.maximum(top, chunk_top)
                weights = jnp.exp2(scores - new_top)
                chunk_total = jnp.sum(weights, axis=0, keepdims=True)
                product = jnp.dot(
                    vbuf[head, slot, :, at : at + KEY_CHUNK],
                    weights.astype(BF16),
                    preferred_element_type=F32,
                )
                if top is None:
                    total, weighted = chunk_total, product
                else:
                    shrink = jnp.exp2(top - new_top)
                    total = total * shrink + chunk_total
                    weighted = weighted * shrink + product
                top = new_top
        result = weighted / total
        log_total = top + jnp.log2(total)
        for slot in range(4):
            part = result[:, slot * GROUP : (slot + 1) * GROUP]
            stat = log_total[:, slot * GROUP : (slot + 1) * GROUP]
            if slot == 0:
                oown[head] = part
                lown[head] = stat
            else:
                osend[head, slot - 1] = part.astype(BF16)
                lsend[head, slot - 1] = jnp.broadcast_to(stat, (8, GROUP))
        back[head] = []
        for slot, d, lands in ((3, 2, 3), (1, -1, 2), (2, 1, 1)):
            back[head].append(send(osend.at[head, slot - 1], orecv.at[head, lands - 1], query_device(d)))
            back[head].append(send(lsend.at[head, slot - 1], lrecv.at[head, lands - 1], query_device(d)))

    guidance = guidance_ref[0]
    swapped = []

    def combine(head):
        for copy in back[head]:
            copy.wait_recv()
        stats = [lown[head]] + [lrecv[head, i, 0:1] for i in range(3)]
        parts = [oown[head]] + [orecv[head, i].astype(F32) for i in range(3)]
        top = functools.reduce(jnp.maximum, stats)
        shares = [jnp.exp2(s - top) for s in stats]
        total = functools.reduce(jnp.add, shares)
        video = functools.reduce(jnp.add, [p * s for p, s in zip(parts, shares)]) / total
        video_log = top + jnp.log2(total)
        halves = []
        for half in range(2):
            text_top = textstat[head, half, 0:1]
            text_total = textstat[head, half, 1:2]
            both = jnp.maximum(video_log, text_top)
            a, b = jnp.exp2(video_log - both), jnp.exp2(text_top - both)
            scale = 1.0 / (a + b * text_total)
            halves.append(video * (a * scale) + textout[head, half] * (b * scale))
        guided = halves[1] + guidance * (halves[0] - halves[1])
        rows = guided.T.astype(BF16)
        abuf[:, head * HD : (head + 1) * HD] = rows[: GROUP // 2]
        asend[head] = rows[GROUP // 2 :]
        swapped.append(
            send(asend.at[head], abuf.at[:, pl.ds(OWN + head * HD, HD)], other)
        )

    send_far(0)
    for head in range(HEADS):
        text_attention(head)
    send_far(1)
    attend(0)
    send_far(2)
    attend(1)
    combine(0)
    attend(2)
    combine(1)
    combine(2)

    for copy in wo_copies:
        copy.wait()
    for copy in swapped:
        copy.wait_recv()
    attention = abuf[...]
    chunks = WIDTH // OUT_CHUNK
    far_sum, near_sum = [], []
    half_rows = ROWS // 2
    for j in range(chunks):
        columns = slice(j * OUT_CHUNK, (j + 1) * OUT_CHUNK)
        product = jnp.dot(attention, wo[:, columns], preferred_element_type=F32)
        pown[j] = product[:ROWS]
        dsend[j] = product[3 * ROWS :].astype(BF16)
        nsend[j, 0] = product[ROWS : 2 * ROWS].astype(BF16)
        nsend[j, 1] = product[2 * ROWS : 3 * ROWS].astype(BF16)
        far_sum.append(
            (
                send(dsend.at[j, low], drecv.at[j, 0], up),
                send(dsend.at[j, high], drecv.at[j, 1], down),
            )
        )
        near_sum.append(send(nsend.at[j, 1, high], nrecv.at[j, 0, high], up))
        near_sum.append(send(nsend.at[j, 0, low], nrecv.at[j, 1, low], down))
    for j in range(chunks):
        for copy in far_sum[j]:
            copy.wait_recv()
        nsend[j, 1, :half_rows] = (
            nsend[j, 1, :half_rows].astype(F32) + drecv[j, 0].astype(F32)
        ).astype(BF16)
        nsend[j, 0, half_rows:] = (
            nsend[j, 0, half_rows:].astype(F32) + drecv[j, 1].astype(F32)
        ).astype(BF16)
        near_sum.append(send(nsend.at[j, 1, low], nrecv.at[j, 0, low], up))
        near_sum.append(send(nsend.at[j, 0, high], nrecv.at[j, 1, high], down))

    xcols_copy.wait()
    position = index_ref[0]
    sigma_step = sigmas_ref[position + 1] - sigmas_ref[position]
    mine = pl.ds(pl.multiple_of(z_hi * ROWS, ROWS), ROWS)
    theirs = pl.ds(pl.multiple_of((1 - z_hi) * ROWS, ROWS), ROWS)
    exchanged = []
    for j in range(chunks):
        for k in (2 * j, 2 * j + 1, 2 * chunks + 2 * j, 2 * chunks + 2 * j + 1):
            near_sum[k].wait_recv()
        guided = pown[j] + nrecv[j, 0].astype(F32) + nrecv[j, 1].astype(F32)
        if j < chunks // 2:
            csend[j] = guided.astype(BF16)
            exchanged.append(send(csend.at[j], crecv.at[j], device(0, 0, 2, 0)))
        else:
            at = (j - chunks // 2) * OUT_CHUNK
            columns = pl.ds(at, OUT_CHUNK)
            guided_ref[mine, columns] = guided.astype(BF16)
            next_ref[mine, columns] = (
                xcols[mine, columns].astype(F32) + sigma_step * guided
            ).astype(BF16)
    for j in range(chunks // 2):
        exchanged[j].wait_recv()
        columns = pl.ds(j * OUT_CHUNK, OUT_CHUNK)
        guided = crecv[j]
        guided_ref[theirs, columns] = guided
        next_ref[theirs, columns] = (
            xcols[theirs, columns].astype(F32) + sigma_step * guided.astype(F32)
        ).astype(BF16)
    for copy in sent:
        copy.wait_send()


def per_device(latents, w_qkv, w_out, q_gain, k_gain, text_kv, text_lengths, sigmas, step_index, guidance):
    any_space = pl.BlockSpec(memory_space=pl.ANY)
    vmem = pl.BlockSpec(memory_space=pltpu.VMEM)
    smem = pl.BlockSpec(memory_space=pltpu.SMEM)
    chunks = WIDTH // OUT_CHUNK
    out = jax.ShapeDtypeStruct((2 * ROWS, HALF), BF16)
    return pl.pallas_call(
        step_kernel,
        name="denoising_step",
        out_shape=(out, out),
        in_specs=[any_space] * 4 + [vmem] * 2 + [smem] * 4,
        out_specs=(vmem, vmem),
        scratch_shapes=[
            pltpu.VMEM((2, 4, ROWS, WIDTH), BF16),
            pltpu.VMEM((WIDTH, 3 * OWN), BF16),
            pltpu.VMEM((2 * OWN, WIDTH), BF16),
            pltpu.VMEM((2, 2, 256, OWN), BF16),
            pltpu.VMEM((2 * ROWS, HALF), BF16),
            pltpu.VMEM((HEADS, 4, GROUP, HD), BF16),
            pltpu.VMEM((HEADS, 4, GROUP, HD), BF16),
            pltpu.VMEM((HEADS, 4, HD, GROUP), BF16),
            pltpu.VMEM((HEADS, GROUP, HD), BF16),
            pltpu.VMEM((HEADS, 2, HD, GROUP), F32),
            pltpu.VMEM((HEADS, 2, 8, GROUP), F32),
            pltpu.VMEM((HEADS, 3, HD, GROUP), BF16),
            pltpu.VMEM((HEADS, 3, HD, GROUP), BF16),
            pltpu.VMEM((HEADS, 3, 8, GROUP), F32),
            pltpu.VMEM((HEADS, 3, 8, GROUP), F32),
            pltpu.VMEM((HEADS, HD, GROUP), F32),
            pltpu.VMEM((HEADS, 1, GROUP), F32),
            pltpu.VMEM((HEADS, GROUP // 2, HD), BF16),
            pltpu.VMEM((GROUP // 2, 2 * OWN), BF16),
            pltpu.VMEM((chunks, ROWS, OUT_CHUNK), BF16),
            pltpu.VMEM((chunks, 2, ROWS // 2, OUT_CHUNK), BF16),
            pltpu.VMEM((chunks, 2, ROWS, OUT_CHUNK), BF16),
            pltpu.VMEM((chunks, 2, ROWS, OUT_CHUNK), BF16),
            pltpu.VMEM((chunks, ROWS, OUT_CHUNK), F32),
            pltpu.VMEM((chunks // 2, ROWS, OUT_CHUNK), BF16),
            pltpu.VMEM((chunks // 2, ROWS, OUT_CHUNK), BF16),
            pltpu.SemaphoreType.DMA((16,)),
            pltpu.SemaphoreType.DMA((MESSAGES,)),
            pltpu.SemaphoreType.DMA((MESSAGES,)),
        ],
        compiler_params=pltpu.CompilerParams(
            collective_id=0, has_side_effects=True, vmem_limit_bytes=60 * 2**20
        ),
        cost_estimate=pl.CostEstimate(
            flops=12 * 10**9, bytes_accessed=15 * 10**6, transcendentals=14 * 10**6
        ),
    )(
        latents,
        jnp.transpose(w_qkv, (1, 0, 2)),
        w_out,
        text_kv,
        q_gain.reshape(1, HD),
        k_gain.reshape(1, HD),
        text_lengths,
        sigmas,
        step_index,
        guidance,
    )


def solution(mesh):
    placed = (
        P(("blk", "ulysses"), None),
        P(None, None, "ulysses"),
        P("ulysses", None),
        P(),
        P(),
        P(None, None, None, "ulysses"),
        P(),
        P(),
        P(),
        P(),
    )
    return jax.shard_map(
        per_device,
        mesh=mesh,
        in_specs=placed,
        out_specs=(P(("blk", "ulysses"), "cfg"), P(("blk", "ulysses"), "cfg")),
        check_vma=False,
    )
```

time: 556 us -> 98.6 us (0.18)
  waiting for transfers between devices: 233 us -> 0 us
  matrix products: 193 us -> 0 us
  Pallas kernels: 0 us -> 92.9 us
  local copies, waits for them, and re-layouts: 79.7 us -> 3.53 us
  other arithmetic: 27.2 us -> 0 us
  between operations: 16.6 us -> 1.93 us
    dot_general x36 -> x0, matrix products: 193 us -> none  [the longest x16 95.3 us: add_keys(): jnp.einsum('hqk,khd->qhd', weights.astype(jnp.bfloat16), values_shaped, p...]
    all_gather x3 -> x0, waiting for transfers between devices: 179 us -> none  [the longest x1 74.4 us: per_device(): lax.all_gather(values_here, 'blk', axis=0, tiled=True)]
    pallas_call x0 -> x1, Pallas kernels: none -> 92.9 us  [per_device(): pl.pallas_call(step_kernel, name='denoising_step', out_shape=(out, out),...]
    dynamic_slice x50 -> x0, local copies, waits for them, and re-layouts: 69.1 us -> none  [the longest x48 67.8 us: fold_keys(): lax.scan(scan_step, carried_state, (key_blocks, value_blocks))]
    reduce_scatter x1 -> x0, waiting for transfers between devices: 38.8 us -> none  [velocity_pair(): lax.psum_scatter(jnp.dot(attention, w_out, preferred_element_type=jnp.flo...]
    reduce_sum x19 -> x0, other arithmetic: 17.7 us -> none  [the longest x16 16.6 us: add_keys(): weight_sum = weight_sum * correction + jnp.sum(weights, axis=2)]
    ppermute x1 -> x0, waiting for transfers between devices: 14.1 us -> none  [partner(): lax.ppermute(array, axis, [(i, i ^ 1 << distance) for i in range(lax.axis...]
  transfers between devices with their start and end apart: 5 -> 0, of which waited for: 5 -> 0; matrix products, arithmetic and copies ran while one was open for 2% -> 0% of each run, Pallas kernels for 0% -> 0%
where the time goes in v1:
time: 98.6 us; the launch traced here: 98.4 us
  Pallas kernels  92.9 us (94%)
  local copies, waits for them, and re-layouts  3.53 us (4%)
  between operations  1.93 us (2%)
    pallas_call x1, Pallas kernels, per_device(): pl.pallas_call(step_kernel, name='denoising_step', out_shape=(out, out),...  92.9 us
    unnamed x2, local copies, waits for them, and re-layouts  3.53 us

profile of v1, /device:TPU:1, one launch (start us, length us, event | category | flops | bytes accessed | tf_op | source)
XLA Modules:
  0.0 98.4 jit_solution(12100982974342453960)
XLA Ops:
  1.9 92.9 %denoising_step.1 = (bf16[128,1536]{1,0:T(8,128)(2,1)}, bf16[128,1536]{1,0:T(8,128)(2,1)}) custom-call(bf16[128,3072]{1,0:T(8,128)(2,1)} %x_hbm.1, bf16[3,3072,768]{2,1,0:T(8,128)(2,1)} %bitcast.3, bf16[768,3072]{1,0:T(8,128)(2,1)} %wout_hbm.1, bf16[2,2,256,768]{3,2,1,0:T(8,128)(2,1)} %text_hbm.1, f32[1,128]{1,0:T(1,128)} %bitcast.4, f32[1,128]{1,0:T(1,128)} %bitcast.5, ...), custom_call_target="tpu_custom_call" | custom-call | flops 12000000000 | bytes 15000000 | tf_op jit(solution)/shard_map/denoising_step/pallas_call | solution.py:431
  94.8 1.8 %copy.16 = bf16[128,1536]{1,0:T(8,128)(2,1)} copy(bf16[128,1536]{1,0:T(8,128)(2,1)} %get-tuple-element.4) | data formatting | bytes 786432
  96.6 1.8 %copy.17 = bf16[128,1536]{1,0:T(8,128)(2,1)} copy(bf16[128,1536]{1,0:T(8,128)(2,1)} %get-tuple-element.5) | data formatting | bytes 786432

commit v2 on v1

v2 whole, which is shorter than its diff:
```python
import functools
import math

import jax
import jax.numpy as jnp
from jax import lax
from jax.experimental import pallas as pl
from jax.experimental.pallas import tpu as pltpu
from jax.sharding import PartitionSpec as P

HD = 128
EPS = 1e-06
LOG2E = math.log2(math.e)
SCORE = LOG2E / math.sqrt(HD)
MESH = pl.DeviceIdType.MESH
NT = (((1,), (1,)), ((), ()))
TN = (((0,), (0,)), ((), ()))
F32 = jnp.float32
BF16 = jnp.bfloat16

HEADS = 3
ROWS = 64
PART = ROWS // 2
UNITS = 4
UNIT = 2 * ROWS
QUERIES = 4 * UNIT
WIDTH = 3072
HALF = WIDTH // 2
OWN = HEADS * HD
MESSAGES = 96


def place():
    blk = lax.axis_index("blk")
    z_hi = lax.axis_index("cfg")
    core = lax.rem(blk, 2)
    x = lax.rem(lax.div(blk, 2), 4)
    z = z_hi * 2 + lax.div(blk, 8)
    return x, lax.axis_index("ulysses"), z, core, z_hi


def step_kernel(
    x_hbm,
    wqkv_hbm,
    wout_hbm,
    text_hbm,
    qgain_ref,
    kgain_ref,
    lengths_ref,
    sigmas_ref,
    index_ref,
    guidance_ref,
    guided_ref,
    next_ref,
    xg,
    wq,
    wo,
    text,
    xcols,
    qs,
    kv,
    qtext,
    textout,
    textstat,
    osend,
    orecv,
    lsend,
    lrecv,
    oown,
    lown,
    asend,
    abuf,
    dsend,
    drecv,
    nsend,
    nrecv,
    local_sem,
    send_sem,
    recv_sem,
):
    x, y, z, core, z_hi = place()

    def device(dx, dy, dz, dc):
        tx = lax.rem(x + dx + 4, 4)
        ty = lax.rem(y + dy + 4, 4)
        tz = lax.rem(z + dz + 4, 4)
        tc = lax.rem(core + dc, 2)
        return (lax.div(tz, 2), lax.rem(tz, 2) * 8 + tx * 2 + tc, ty)

    def key_device(d):
        return device((1 - core) * d, 0, core * d, 0)

    def query_device(d):
        return device(core * d, 0, (1 - core) * d, 0)

    locals_started = []

    def local(src, dst):
        copy = pltpu.make_async_copy(src, dst, local_sem.at[len(locals_started)])
        copy.start()
        locals_started.append(copy)
        return copy

    own_rows = x_hbm.at[pl.ds(pl.multiple_of(z_hi * ROWS, ROWS), ROWS)]
    own_copy = local(own_rows, xg.at[0, 0])
    own_col = pl.multiple_of(core * OWN, OWN)
    w_copies = [
        local(wqkv_hbm.at[which, :, pl.ds(own_col, OWN)], wq.at[:, pl.ds(at * OWN, OWN)])
        for at, which in enumerate((1, 2, 0))
    ]
    text_copy = local(text_hbm.at[:, :, :, pl.ds(own_col, OWN)], text)
    columns_here = pl.ds(pl.multiple_of(z_hi * HALF, HALF), HALF)
    wo_copies = [
        local(wout_hbm.at[pl.ds(pl.multiple_of(c * OWN, OWN), OWN), columns_here], wo.at[pl.ds(at * OWN, OWN)])
        for at, c in enumerate((core, 1 - core))
    ]
    xcols_copy = local(x_hbm.at[:, columns_here], xcols)

    barrier = pltpu.get_barrier_semaphore()
    greeted = [
        (0, 1, 0, 0),
        (0, -1, 0, 0),
        (0, 0, 0, 1),
        (1, 0, 0, 0),
        (-1, 0, 0, 0),
        (2, 0, 0, 0),
        (0, 0, 1, 0),
        (0, 0, -1, 0),
        (0, 0, 2, 0),
        (0, 0, 2, 1),
    ]
    for offset in greeted:
        pl.semaphore_signal(barrier, inc=1, device_id=device(*offset), device_id_type=MESH)
    pl.semaphore_wait(barrier, len(greeted))

    sent = []

    def send(src, dst, to):
        number = len(sent)
        copy = pltpu.make_async_remote_copy(
            src_ref=src,
            dst_ref=dst,
            send_sem=send_sem.at[number],
            recv_sem=recv_sem.at[number],
            device_id=to,
            device_id_type=MESH,
        )
        copy.start()
        sent.append(copy)
        return copy

    up, down, other = device(0, 1, 0, 0), device(0, -1, 0, 0), device(0, 0, 0, 1)
    low, high = pl.ds(0, PART), pl.ds(PART, PART)

    def own_part(part):
        return x_hbm.at[pl.ds(pl.multiple_of(z_hi * ROWS + part * PART, PART), PART)]

    up_first = send(own_part(0), xg.at[1, 0, low], up)
    down_first = send(own_part(1), xg.at[1, 0, high], down)
    across = [send(own_rows, xg.at[0, 1], other)]
    up_second = send(own_part(1), xg.at[2, 0, low], up)
    down_second = send(own_part(0), xg.at[2, 0, high], down)

    def normed(value, gain):
        mean_square = jnp.mean(value * value, axis=1, keepdims=True)
        return value * lax.rsqrt(mean_square + EPS) * gain

    def project(unit):
        product = jnp.dot(
            xg[unit].reshape(UNIT, WIDTH), wq[...], preferred_element_type=F32
        )
        for head in range(HEADS):
            at = head * HD
            key = normed(product[:, at : at + HD], kgain_ref[...])
            kv[0, unit, 0, head] = key.astype(BF16)
            kv[0, unit, 1, head] = product[:, OWN + at : OWN + at + HD].T.astype(BF16)
            query = normed(product[:, 2 * OWN + at : 2 * OWN + at + HD], qgain_ref[...])
            qtext[unit, head] = query.astype(BF16)
            qs[0, unit, head] = (query * SCORE).astype(BF16)

    near_kv, near_q, far_kv, far_q = {}, {}, {}, {}

    def send_near_kv(unit):
        near_kv[unit] = [
            send(kv.at[0, unit], kv.at[1, unit], key_device(1)),
            send(kv.at[0, unit], kv.at[2, unit], key_device(-1)),
        ]

    def send_near_q(unit):
        near_q[unit] = [
            send(qs.at[0, unit], qs.at[1, unit], query_device(1)),
            send(qs.at[0, unit], qs.at[2, unit], query_device(-1)),
        ]

    def send_far_kv(unit):
        for copy in near_kv[unit]:
            copy.wait_recv()
        far_kv[unit] = [
            send(kv.at[1, unit, 0], kv.at[3, unit, 0], key_device(1)),
            send(kv.at[2, unit, 1], kv.at[3, unit, 1], key_device(-1)),
        ]

    def send_far_q(unit):
        for copy in near_q[unit]:
            copy.wait_recv()
        first, second = pl.ds(0, UNIT // 2), pl.ds(UNIT // 2, UNIT // 2)
        far_q[unit] = [
            send(qs.at[1, unit, :, first], qs.at[3, unit, :, first], query_device(1)),
            send(qs.at[2, unit, :, second], qs.at[3, unit, :, second], query_device(-1)),
        ]

    lsend[...] = jnp.zeros_like(lsend)
    for copy in w_copies:
        copy.wait()
    own_copy.wait()
    across[0].wait_recv()
    project(0)
    send_near_kv(0)
    send_near_q(0)
    up_first.wait_recv()
    far_up = send(xg.at[1, 0, low], xg.at[3, 0, low], up)
    down_first.wait_recv()
    far_down = send(xg.at[1, 0, high], xg.at[3, 0, high], down)
    across.append(send(xg.at[1, 0], xg.at[1, 1], other))
    send_far_kv(0)
    send_far_q(0)
    across[1].wait_recv()
    project(1)
    send_near_kv(1)
    send_near_q(1)
    up_second.wait_recv()
    down_second.wait_recv()
    across.append(send(xg.at[2, 0], xg.at[2, 1], other))
    across[2].wait_recv()
    project(2)
    send_near_kv(2)
    far_up.wait_recv()
    far_down.wait_recv()
    across.append(send(xg.at[3, 0], xg.at[3, 1], other))
    send_far_kv(1)
    across[3].wait_recv()
    project(3)
    send_near_kv(3)
    send_near_q(3)
    send_far_q(1)
    send_far_kv(2)

    def text_attention(head):
        columns = slice(head * HD, (head + 1) * HD)
        queries = qtext[:, head].reshape(UNITS * UNIT, HD)
        for half in range(2):
            scores = (
                lax.dot_general(text[half, 0, :, columns], queries, NT, preferred_element_type=F32)
                * SCORE
            )
            valid = lax.broadcasted_iota(jnp.int32, scores.shape, 0) < lengths_ref[half]
            scores = jnp.where(valid, scores, -jnp.inf)
            top = jnp.max(scores, axis=0, keepdims=True)
            weights = jnp.exp2(scores - top)
            total = jnp.sum(weights, axis=0, keepdims=True)
            textout[head, half] = lax.dot_general(
                text[half, 1, :, columns], weights.astype(BF16), TN, preferred_element_type=F32
            )
            textstat[head, half, 0:1] = top
            textstat[head, half, 1:2] = total

    back = {unit: [] for unit in range(UNITS)}

    def attend(unit, heads=range(HEADS)):
        steps = [(head, pair) for head in heads for pair in range(2)]
        scores_of = {}

        def score(head, pair):
            keys = kv[2 * pair : 2 * pair + 2, :, 0, head].reshape(2 * UNITS * UNIT, HD)
            queries = qs[:, unit, head].reshape(QUERIES, HD)
            return lax.dot_general(keys, queries, NT, preferred_element_type=F32)

        scores_of[steps[0]] = score(*steps[0])
        for i, (head, pair) in enumerate(steps):
            if i + 1 < len(steps):
                scores_of[steps[i + 1]] = score(*steps[i + 1])
            scores = scores_of.pop((head, pair))
            new_top = jnp.max(scores, axis=0, keepdims=True)
            if pair:
                new_top = jnp.maximum(new_top, top)
            weights = jnp.exp2(scores - new_top)
            part_total = jnp.sum(weights, axis=0, keepdims=True)
            values = jnp.concatenate(
                [kv[slot, u, 1, head] for slot in (2 * pair, 2 * pair + 1) for u in range(UNITS)], axis=1
            )
            product = jnp.dot(values, weights.astype(BF16), preferred_element_type=F32)
            if pair:
                shrink = jnp.exp2(top - new_top)
                part_total = total * shrink + part_total
                product = weighted * shrink + product
            top, total, weighted = new_top, part_total, product
            if pair:
                result = weighted / total
                log_total = top + jnp.log2(total)
                for slot in range(4):
                    part = result[:, slot * UNIT : (slot + 1) * UNIT]
                    stat = log_total[:, slot * UNIT : (slot + 1) * UNIT]
                    if slot == 0:
                        oown[unit, head] = part
                        lown[unit, head : head + 1] = stat
                    else:
                        osend[unit, slot - 1, head] = part.astype(BF16)
                        lsend[unit, slot - 1, head : head + 1] = stat

    def send_back(unit):
        for slot, d, lands in ((3, 2, 3), (1, -1, 2), (2, 1, 1)):
            back[unit].append(send(osend.at[unit, slot - 1], orecv.at[unit, lands - 1], query_device(d)))
            back[unit].append(send(lsend.at[unit, slot - 1], lrecv.at[unit, lands - 1], query_device(d)))

    guidance = guidance_ref[0]
    swapped = {}

    def combine(unit):
        for copy in back[unit]:
            copy.wait_recv()
        span = slice(unit * UNIT, (unit + 1) * UNIT)
        for head in range(HEADS):
            stats = [lown[unit, head : head + 1]] + [lrecv[unit, i, head : head + 1] for i in range(3)]
            parts = [oown[unit, head]] + [orecv[unit, i, head].astype(F32) for i in range(3)]
            top = functools.reduce(jnp.maximum, stats)
            shares = [jnp.exp2(s - top) for s in stats]
            total = functools.reduce(jnp.add, shares)
            video = functools.reduce(jnp.add, [p * s for p, s in zip(parts, shares)]) / total
            video_log = top + jnp.log2(total)
            halves = []
            for half in range(2):
                text_top = textstat[head, half, 0:1, span]
                text_total = textstat[head, half, 1:2, span]
                both = jnp.maximum(video_log, text_top)
                a, b = jnp.exp2(video_log - both), jnp.exp2(text_top - both)
                scale = 1.0 / (a + b * text_total)
                halves.append(video * (a * scale) + textout[head, half, :, span] * (b * scale))
            guided = halves[1] + guidance * (halves[0] - halves[1])
            rows = guided.T.astype(BF16)
            columns = slice(head * HD, (head + 1) * HD)
            asend[unit, 0, :, columns] = rows[:ROWS]
            asend[unit, 1, :, columns] = rows[ROWS:]
        abuf[unit, 0, :, :OWN] = asend[unit, 0]
        first, second = pl.ds(0, OWN), pl.ds(OWN, OWN)
        swapped[unit] = [
            send(asend.at[unit, 0], abuf.at[unit, 1, :, first], device(0, 0, 2, 0)),
            send(asend.at[unit, 1], abuf.at[unit, 1, :, second], device(0, 0, 2, 1)),
            send(asend.at[unit, 1], abuf.at[unit, 0, :, second], other),
        ]

    def output(unit):
        for copy in swapped[unit]:
            copy.wait_recv()
        return jnp.dot(
            abuf[unit].reshape(UNIT, 2 * OWN), wo[...], preferred_element_type=F32
        ).reshape(2, ROWS, HALF)

    text_copy.wait()
    for head in range(HEADS):
        text_attention(head)
    send_far_kv(3)
    send_far_q(3)
    send_near_q(2)
    for unit in range(UNITS):
        for copy in far_kv[unit]:
            copy.wait_recv()
    for copy in far_q[3]:
        copy.wait_recv()
    attend(3)
    send_back(3)
    send_far_q(2)
    for copy in far_q[1]:
        copy.wait_recv()
    attend(1)
    send_back(1)
    combine(3)
    for copy in far_q[2]:
        copy.wait_recv()
    attend(2)
    send_back(2)
    for copy in wo_copies:
        copy.wait()
    dsend[...] = output(3).astype(BF16)
    far_sum = [
        send(dsend.at[:, low], drecv.at[0], up),
        send(dsend.at[:, high], drecv.at[1], down),
    ]
    combine(1)
    for copy in far_q[0]:
        copy.wait_recv()
    attend(0, (0, 1))
    nsend[0] = output(1).astype(BF16)
    near_sum = [
        send(nsend.at[0, :, low], nrecv.at[0, :, low], down),
        send(nsend.at[0, :, high], nrecv.at[1, :, high], up),
    ]
    combine(2)
    attend(0, (2,))
    send_back(0)
    product = output(2)
    for copy in far_sum:
        copy.wait_recv()
    nsend[1, :, :PART] = (product[:, :PART] + drecv[1].astype(F32)).astype(BF16)
    nsend[1, :, PART:] = (product[:, PART:] + drecv[0].astype(F32)).astype(BF16)
    near_sum += [
        send(nsend.at[1, :, low], nrecv.at[0, :, high], down),
        send(nsend.at[1, :, high], nrecv.at[1, :, low], up),
    ]
    combine(0)
    xcols_copy.wait()
    position = index_ref[0]
    sigma_step = sigmas_ref[position + 1] - sigmas_ref[position]
    product = output(0)
    for copy in near_sum:
        copy.wait_recv()
    guided = product + nrecv[0].astype(F32) + nrecv[1].astype(F32)
    for at, half in enumerate((z_hi, 1 - z_hi)):
        rows = pl.ds(pl.multiple_of(half * ROWS, ROWS), ROWS)
        guided_ref[rows] = guided[at].astype(BF16)
        next_ref[rows] = (xcols[rows].astype(F32) + sigma_step * guided[at]).astype(BF16)
    for copy in sent:
        copy.wait_send()


def per_device(latents, w_qkv, w_out, q_gain, k_gain, text_kv, text_lengths, sigmas, step_index, guidance):
    any_space = pl.BlockSpec(memory_space=pl.ANY)
    vmem = pl.BlockSpec(memory_space=pltpu.VMEM)
    smem = pl.BlockSpec(memory_space=pltpu.SMEM)
    out = jax.ShapeDtypeStruct((2 * ROWS, HALF), BF16)
    return pl.pallas_call(
        step_kernel,
        name="denoising_step",
        out_shape=(out, out),
        in_specs=[any_space] * 4 + [vmem] * 2 + [smem] * 4,
        out_specs=(vmem, vmem),
        scratch_shapes=[
            pltpu.VMEM((UNITS, 2, ROWS, WIDTH), BF16),
            pltpu.VMEM((WIDTH, 3 * OWN), BF16),
            pltpu.VMEM((2 * OWN, HALF), BF16),
            pltpu.VMEM((2, 2, 256, OWN), BF16),
            pltpu.VMEM((2 * ROWS, HALF), BF16),
            pltpu.VMEM((4, UNITS, HEADS, UNIT, HD), BF16),
            pltpu.VMEM((4, UNITS, 2, HEADS, UNIT, HD), BF16),
            pltpu.VMEM((UNITS, HEADS, UNIT, HD), BF16),
            pltpu.VMEM((HEADS, 2, HD, UNITS * UNIT), F32),
            pltpu.VMEM((HEADS, 2, 8, UNITS * UNIT), F32),
            pltpu.VMEM((UNITS, 3, HEADS, HD, UNIT), BF16),
            pltpu.VMEM((UNITS, 3, HEADS, HD, UNIT), BF16),
            pltpu.VMEM((UNITS, 3, 8, UNIT), F32),
            pltpu.VMEM((UNITS, 3, 8, UNIT), F32),
            pltpu.VMEM((UNITS, HEADS, HD, UNIT), F32),
            pltpu.VMEM((UNITS, 8, UNIT), F32),
            pltpu.VMEM((UNITS, 2, ROWS, OWN), BF16),
            pltpu.VMEM((UNITS, 2, ROWS, 2 * OWN), BF16),
            pltpu.VMEM((2, ROWS, HALF), BF16),
            pltpu.VMEM((2, 2, PART, HALF), BF16),
            pltpu.VMEM((2, 2, ROWS, HALF), BF16),
            pltpu.VMEM((2, 2, ROWS, HALF), BF16),
            pltpu.SemaphoreType.DMA((16,)),
            pltpu.SemaphoreType.DMA((MESSAGES,)),
            pltpu.SemaphoreType.DMA((MESSAGES,)),
        ],
        compiler_params=pltpu.CompilerParams(
            collective_id=0, has_side_effects=True, vmem_limit_bytes=60 * 2**20
        ),
        cost_estimate=pl.CostEstimate(
            flops=12 * 10**9, bytes_accessed=15 * 10**6, transcendentals=14 * 10**6
        ),
    )(
        latents,
        jnp.transpose(w_qkv, (1, 0, 2)),
        w_out,
        text_kv,
        q_gain.reshape(1, HD),
        k_gain.reshape(1, HD),
        text_lengths,
        sigmas,
        step_index,
        guidance,
    )


def solution(mesh):
    placed = (
        P(("blk", "ulysses"), None),
        P(None, None, "ulysses"),
        P("ulysses", None),
        P(),
        P(),
        P(None, None, None, "ulysses"),
        P(),
        P(),
        P(),
        P(),
    )
    return jax.shard_map(
        per_device,
        mesh=mesh,
        in_specs=placed,
        out_specs=(P(("blk", "ulysses"), "cfg"), P(("blk", "ulysses"), "cfg")),
        check_vma=False,
    )
```

time: 98.6 us -> 80 us (0.81)
  Pallas kernels: 92.9 us -> 74.3 us
    pallas_call x1, Pallas kernels: 92.9 us -> 74.3 us  [per_device(): pl.pallas_call(step_kernel, name='denoising_step', out_shape=(out, out),...]
where the time goes in v2:
time: 80 us; the launch traced here: 79.8 us
  Pallas kernels  74.3 us (93%)
  local copies, waits for them, and re-layouts  3.53 us (4%)
  between operations  1.93 us (2%)
    pallas_call x1, Pallas kernels, per_device(): pl.pallas_call(step_kernel, name='denoising_step', out_shape=(out, out),...  74.3 us
    unnamed x2, local copies, waits for them, and re-layouts  3.53 us

profile of v2, /device:TPU:1, one launch (start us, length us, event | category | flops | bytes accessed | tf_op | source)
XLA Modules:
  0.0 79.8 jit_solution(4389952629312243063)
XLA Ops:
  1.9 74.3 %denoising_step.1 = (bf16[128,1536]{1,0:T(8,128)(2,1)}, bf16[128,1536]{1,0:T(8,128)(2,1)}) custom-call(bf16[128,3072]{1,0:T(8,128)(2,1)} %x_hbm.1, bf16[3,3072,768]{2,1,0:T(8,128)(2,1)} %bitcast.3, bf16[768,3072]{1,0:T(8,128)(2,1)} %wout_hbm.1, bf16[2,2,256,768]{3,2,1,0:T(8,128)(2,1)} %text_hbm.1, f32[1,128]{1,0:T(1,128)} %bitcast.4, f32[1,128]{1,0:T(1,128)} %bitcast.5, ...), custom_call_target="tpu_custom_call" | custom-call | flops 12000000000 | bytes 15000000 | tf_op jit(solution)/shard_map/denoising_step/pallas_call | solution.py:430
  76.3 1.8 %copy.16 = bf16[128,1536]{1,0:T(8,128)(2,1)} copy(bf16[128,1536]{1,0:T(8,128)(2,1)} %get-tuple-element.4) | data formatting | bytes 786432
  78.0 1.8 %copy.17 = bf16[128,1536]{1,0:T(8,128)(2,1)} copy(bf16[128,1536]{1,0:T(8,128)(2,1)} %get-tuple-element.5) | data formatting | bytes 786432

commit v3 on v2

--- a/solution.py
+++ b/solution.py
@@ -27,7 +27,9 @@
 WIDTH = 3072
 HALF = WIDTH // 2
 OWN = HEADS * HD
-MESSAGES = 96
+STAT = 16
+SUM_COLUMNS = 768
+MESSAGES = 128
 
 
 def place():
@@ -64,8 +66,6 @@
     textstat,
     osend,
     orecv,
-    lsend,
-    lrecv,
     oown,
     lown,
     asend,
@@ -209,7 +209,6 @@
             send(qs.at[2, unit, :, second], qs.at[3, unit, :, second], query_device(-1)),
         ]
 
-    lsend[...] = jnp.zeros_like(lsend)
     for copy in w_copies:
         copy.wait()
     own_copy.wait()
@@ -222,27 +221,27 @@
     down_first.wait_recv()
     far_down = send(xg.at[1, 0, high], xg.at[3, 0, high], down)
     across.append(send(xg.at[1, 0], xg.at[1, 1], other))
-    send_far_kv(0)
-    send_far_q(0)
     across[1].wait_recv()
     project(1)
     send_near_kv(1)
     send_near_q(1)
+    send_far_kv(0)
+    send_far_q(0)
     up_second.wait_recv()
     down_second.wait_recv()
     across.append(send(xg.at[2, 0], xg.at[2, 1], other))
     across[2].wait_recv()
     project(2)
     send_near_kv(2)
+    send_far_kv(1)
+    send_far_q(1)
     far_up.wait_recv()
     far_down.wait_recv()
     across.append(send(xg.at[3, 0], xg.at[3, 1], other))
-    send_far_kv(1)
     across[3].wait_recv()
     project(3)
     send_near_kv(3)
     send_near_q(3)
-    send_far_q(1)
     send_far_kv(2)
 
     def text_attention(head):
@@ -264,9 +263,9 @@
             textstat[head, half, 0:1] = top
             textstat[head, half, 1:2] = total
 
-    back = {unit: [] for unit in range(UNITS)}
-
-    def attend(unit, heads=range(HEADS)):
+    back = {}
+
+    def attend(unit, heads, sends):
         steps = [(head, pair) for head in heads for pair in range(2)]
         scores_of = {}
 
@@ -276,9 +275,9 @@
             return lax.dot_general(keys, queries, NT, preferred_element_type=F32)
 
         scores_of[steps[0]] = score(*steps[0])
-        for i, (head, pair) in enumerate(steps):
-            if i + 1 < len(steps):
-                scores_of[steps[i + 1]] = score(*steps[i + 1])
+        for n, (head, pair) in enumerate(steps):
+            if n + 1 < len(steps):
+                scores_of[steps[n + 1]] = score(*steps[n + 1])
             scores = scores_of.pop((head, pair))
             new_top = jnp.max(scores, axis=0, keepdims=True)
             if pair:
@@ -294,34 +293,50 @@
                 part_total = total * shrink + part_total
                 product = weighted * shrink + product
             top, total, weighted = new_top, part_total, product
-            if pair:
-                result = weighted / total
-                log_total = top + jnp.log2(total)
-                for slot in range(4):
-                    part = result[:, slot * UNIT : (slot + 1) * UNIT]
-                    stat = log_total[:, slot * UNIT : (slot + 1) * UNIT]
-                    if slot == 0:
-                        oown[unit, head] = part
-                        lown[unit, head : head + 1] = stat
-                    else:
-                        osend[unit, slot - 1, head] = part.astype(BF16)
-                        lsend[unit, slot - 1, head : head + 1] = stat
-
-    def send_back(unit):
-        for slot, d, lands in ((3, 2, 3), (1, -1, 2), (2, 1, 1)):
-            back[unit].append(send(osend.at[unit, slot - 1], orecv.at[unit, lands - 1], query_device(d)))
-            back[unit].append(send(lsend.at[unit, slot - 1], lrecv.at[unit, lands - 1], query_device(d)))
+            if not pair:
+                continue
+            result = weighted / total
+            log_total = top + jnp.log2(total)
+            row = lax.broadcasted_iota(jnp.int32, (STAT, UNIT), 0)
+            for slot in range(4):
+                part = result[:, slot * UNIT : (slot + 1) * UNIT]
+                stat = log_total[:, slot * UNIT : (slot + 1) * UNIT]
+                if slot == 0:
+                    oown[unit, head] = part
+                    lown[unit, head : head + 1] = stat
+                else:
+                    first = stat.astype(BF16).astype(F32)
+                    second = (stat - first).astype(BF16).astype(F32)
+                    third = stat - first - second
+                    osend[unit, slot - 1, head, :HD] = part.astype(BF16)
+                    osend[unit, slot - 1, head, HD:] = jnp.where(
+                        row == 0, first, jnp.where(row == 1, second, third)
+                    ).astype(BF16)
+            for group in sends:
+                if head == group[-1]:
+                    send_back(unit, group)
+
+    def send_back(unit, group):
+        span = pl.ds(group[0], len(group))
+        back[unit, group] = [
+            send(osend.at[unit, slot - 1, span], orecv.at[unit, lands - 1, span], query_device(d))
+            for slot, d, lands in ((3, 2, 3), (1, -1, 2), (2, 1, 1))
+        ]
 
     guidance = guidance_ref[0]
-    swapped = {}
-
-    def combine(unit):
-        for copy in back[unit]:
+    swapped = {unit: [] for unit in range(UNITS)}
+
+    def combine(unit, group):
+        for copy in back[unit, group]:
             copy.wait_recv()
         span = slice(unit * UNIT, (unit + 1) * UNIT)
-        for head in range(HEADS):
-            stats = [lown[unit, head : head + 1]] + [lrecv[unit, i, head : head + 1] for i in range(3)]
-            parts = [oown[unit, head]] + [orecv[unit, i, head].astype(F32) for i in range(3)]
+        for head in group:
+            stats = [lown[unit, head : head + 1]]
+            parts = [oown[unit, head]]
+            for i in range(3):
+                log_parts = orecv[unit, i, head, HD:].astype(F32)
+                stats.append(log_parts[0:1] + log_parts[1:2] + log_parts[2:3])
+                parts.append(orecv[unit, i, head, :HD].astype(F32))
             top = functools.reduce(jnp.maximum, stats)
             shares = [jnp.exp2(s - top) for s in stats]
             total = functools.reduce(jnp.add, shares)
@@ -338,14 +353,15 @@
             guided = halves[1] + guidance * (halves[0] - halves[1])
             rows = guided.T.astype(BF16)
             columns = slice(head * HD, (head + 1) * HD)
+            abuf[unit, 0, :, columns] = rows[:ROWS]
             asend[unit, 0, :, columns] = rows[:ROWS]
             asend[unit, 1, :, columns] = rows[ROWS:]
-        abuf[unit, 0, :, :OWN] = asend[unit, 0]
-        first, second = pl.ds(0, OWN), pl.ds(OWN, OWN)
-        swapped[unit] = [
-            send(asend.at[unit, 0], abuf.at[unit, 1, :, first], device(0, 0, 2, 0)),
-            send(asend.at[unit, 1], abuf.at[unit, 1, :, second], device(0, 0, 2, 1)),
-            send(asend.at[unit, 1], abuf.at[unit, 0, :, second], other),
+        here = pl.ds(group[0] * HD, len(group) * HD)
+        there = pl.ds(OWN + group[0] * HD, len(group) * HD)
+        swapped[unit] += [
+            send(asend.at[unit, 0, :, here], abuf.at[unit, 1, :, here], device(0, 0, 2, 0)),
+            send(asend.at[unit, 1, :, here], abuf.at[unit, 1, :, there], device(0, 0, 2, 1)),
+            send(asend.at[unit, 1, :, here], abuf.at[unit, 0, :, there], other),
         ]
 
     def output(unit):
@@ -361,52 +377,58 @@
     send_far_kv(3)
     send_far_q(3)
     send_near_q(2)
+    def arrived(copies):
+        for copy in copies:
+            copy.wait_recv()
+
+    every = (0, 1, 2)
     for unit in range(UNITS):
-        for copy in far_kv[unit]:
-            copy.wait_recv()
-    for copy in far_q[3]:
-        copy.wait_recv()
-    attend(3)
-    send_back(3)
+        arrived(far_kv[unit])
+    arrived(far_q[3])
+    attend(3, every, sends=(every,))
     send_far_q(2)
-    for copy in far_q[1]:
-        copy.wait_recv()
-    attend(1)
-    send_back(1)
-    combine(3)
-    for copy in far_q[2]:
-        copy.wait_recv()
-    attend(2)
-    send_back(2)
+    arrived(far_q[1])
+    attend(1, every, sends=(every,))
+    combine(3, every)
+    arrived(far_q[2])
+    attend(2, every, sends=(every,))
     for copy in wo_copies:
         copy.wait()
     dsend[...] = output(3).astype(BF16)
+    cuts = [pl.ds(at, SUM_COLUMNS) for at in range(0, HALF, SUM_COLUMNS)]
     far_sum = [
-        send(dsend.at[:, low], drecv.at[0], up),
-        send(dsend.at[:, high], drecv.at[1], down),
+        (
+            send(dsend.at[:, low, cut], drecv.at[0, :, :, cut], up),
+            send(dsend.at[:, high, cut], drecv.at[1, :, :, cut], down),
+        )
+        for cut in cuts
     ]
-    combine(1)
-    for copy in far_q[0]:
-        copy.wait_recv()
-    attend(0, (0, 1))
+    combine(1, every)
+    arrived(far_q[0])
+    attend(0, (0, 1), sends=((0, 1),))
     nsend[0] = output(1).astype(BF16)
     near_sum = [
         send(nsend.at[0, :, low], nrecv.at[0, :, low], down),
         send(nsend.at[0, :, high], nrecv.at[1, :, high], up),
     ]
-    combine(2)
-    attend(0, (2,))
-    send_back(0)
+    combine(2, every)
+    attend(0, (2,), sends=((2,),))
     product = output(2)
-    for copy in far_sum:
-        copy.wait_recv()
-    nsend[1, :, :PART] = (product[:, :PART] + drecv[1].astype(F32)).astype(BF16)
-    nsend[1, :, PART:] = (product[:, PART:] + drecv[0].astype(F32)).astype(BF16)
-    near_sum += [
-        send(nsend.at[1, :, low], nrecv.at[0, :, high], down),
-        send(nsend.at[1, :, high], nrecv.at[1, :, low], up),
-    ]
-    combine(0)
+    for copies, cut in zip(far_sum, cuts):
+        arrived(copies)
+        columns = slice(cut.start, cut.start + SUM_COLUMNS)
+        nsend[1, :, :PART, columns] = (
+            product[:, :PART, columns] + drecv[1, :, :, columns].astype(F32)
+        ).astype(BF16)
+        nsend[1, :, PART:, columns] = (
+            product[:, PART:, columns] + drecv[0, :, :, columns].astype(F32)
+        ).astype(BF16)
+        near_sum += [
+            send(nsend.at[1, :, low, cut], nrecv.at[0, :, high, cut], down),
+            send(nsend.at[1, :, high, cut], nrecv.at[1, :, low, cut], up),
+        ]
+    combine(0, (0, 1))
+    combine(0, (2,))
     xcols_copy.wait()
     position = index_ref[0]
     sigma_step = sigmas_ref[position + 1] - sigmas_ref[position]
@@ -422,12 +444,17 @@
         copy.wait_send()
 
 
+def hand_over(guided_ref, next_ref, guided_out, next_out):
+    guided_out[...] = guided_ref[...]
+    next_out[...] = next_ref[...]
+
+
 def per_device(latents, w_qkv, w_out, q_gain, k_gain, text_kv, text_lengths, sigmas, step_index, guidance):
     any_space = pl.BlockSpec(memory_space=pl.ANY)
     vmem = pl.BlockSpec(memory_space=pltpu.VMEM)
     smem = pl.BlockSpec(memory_space=pltpu.SMEM)
     out = jax.ShapeDtypeStruct((2 * ROWS, HALF), BF16)
-    return pl.pallas_call(
+    guided, latents_after = pl.pallas_call(
         step_kernel,
         name="denoising_step",
         out_shape=(out, out),
@@ -444,10 +471,8 @@
             pltpu.VMEM((UNITS, HEADS, UNIT, HD), BF16),
             pltpu.VMEM((HEADS, 2, HD, UNITS * UNIT), F32),
             pltpu.VMEM((HEADS, 2, 8, UNITS * UNIT), F32),
-            pltpu.VMEM((UNITS, 3, HEADS, HD, UNIT), BF16),
-            pltpu.VMEM((UNITS, 3, HEADS, HD, UNIT), BF16),
-            pltpu.VMEM((UNITS, 3, 8, UNIT), F32),
-            pltpu.VMEM((UNITS, 3, 8, UNIT), F32),
+            pltpu.VMEM((UNITS, 3, HEADS, HD + STAT, UNIT), BF16),
+            pltpu.VMEM((UNITS, 3, HEADS, HD + STAT, UNIT), BF16),
             pltpu.VMEM((UNITS, HEADS, HD, UNIT), F32),
             pltpu.VMEM((UNITS, 8, UNIT), F32),
             pltpu.VMEM((UNITS, 2, ROWS, OWN), BF16),
@@ -478,6 +503,9 @@
         step_index,
         guidance,
     )
+    return pl.pallas_call(
+        hand_over, name="hand_over", out_shape=(out, out), in_specs=[vmem, vmem], out_specs=(vmem, vmem)
+    )(guided, latents_after)
 
 
 def solution(mesh):

time: 80 us -> 78.3 us (0.979)
  local copies, waits for them, and re-layouts: 3.53 us -> 0 us
  Pallas kernels: 74.3 us -> 76.2 us
    unnamed x2 -> x0, local copies, waits for them, and re-layouts: 3.53 us -> none
    pallas_call x0 -> x1, Pallas kernels: none -> 2.02 us  [per_device(): pl.pallas_call(hand_over, name='hand_over', out_shape=(out, out), in_spec...]
where the time goes in v3:
time: 78.3 us; the launch traced here: 78.1 us
  Pallas kernels  76.2 us (97%)
  between operations  1.93 us (2%)
    pallas_call x1, Pallas kernels, per_device(): pl.pallas_call(step_kernel, name='denoising_step', out_shape=(out, out),...  74.2 us
    pallas_call x1, Pallas kernels, per_device(): pl.pallas_call(hand_over, name='hand_over', out_shape=(out, out), in_spec...  2.02 us

profile of v3, /device:TPU:1, one launch (start us, length us, event | category | flops | bytes accessed | tf_op | source)
XLA Modules:
  0.0 78.1 jit_solution(3743299136085999891)
XLA Ops:
  1.9 74.2 %denoising_step.1 = (bf16[128,1536]{1,0:T(8,128)(2,1)}, bf16[128,1536]{1,0:T(8,128)(2,1)}) custom-call(bf16[128,3072]{1,0:T(8,128)(2,1)} %x_hbm.1, bf16[3,3072,768]{2,1,0:T(8,128)(2,1)} %bitcast.3, bf16[768,3072]{1,0:T(8,128)(2,1)} %wout_hbm.1, bf16[2,2,256,768]{3,2,1,0:T(8,128)(2,1)} %text_hbm.1, f32[1,128]{1,0:T(1,128)} %bitcast.4, f32[1,128]{1,0:T(1,128)} %bitcast.5, ...), custom_call_target="tpu_custom_call" | custom-call | flops 12000000000 | bytes 15000000 | tf_op jit(solution)/shard_map/denoising_step/pallas_call | solution.py:457
  76.1 2.0 %hand_over.1 = (bf16[128,1536]{1,0:T(8,128)(2,1)}, bf16[128,1536]{1,0:T(8,128)(2,1)}) custom-call(bf16[128,1536]{1,0:T(8,128)(2,1)} %get-tuple-element.4.guided_ref, bf16[128,1536]{1,0:T(8,128)(2,1)} %get-tuple-element.5.next_ref), custom_call_target="tpu_custom_call" | custom-call | tf_op jit(solution)/shard_map/hand_over/pallas_call | solution.py:506

commit v4 on v3

--- a/solution.py
+++ b/solution.py
@@ -376,7 +376,6 @@
         text_attention(head)
     send_far_kv(3)
     send_far_q(3)
-    send_near_q(2)
     def arrived(copies):
         for copy in copies:
             copy.wait_recv()
@@ -385,11 +384,15 @@
     for unit in range(UNITS):
         arrived(far_kv[unit])
     arrived(far_q[3])
-    attend(3, every, sends=(every,))
+    send_near_q(2)
+    attend(3, every, sends=((0, 1), (2,)))
     send_far_q(2)
     arrived(far_q[1])
-    attend(1, every, sends=(every,))
-    combine(3, every)
+    attend(1, (0, 1), sends=())
+    combine(3, (0, 1))
+    combine(3, (2,))
+    attend(1, (2,), sends=())
+    send_back(1, every)
     arrived(far_q[2])
     attend(2, every, sends=(every,))
     for copy in wo_copies:
@@ -406,13 +409,14 @@
     combine(1, every)
     arrived(far_q[0])
     attend(0, (0, 1), sends=((0, 1),))
+    combine(2, every)
     nsend[0] = output(1).astype(BF16)
     near_sum = [
         send(nsend.at[0, :, low], nrecv.at[0, :, low], down),
         send(nsend.at[0, :, high], nrecv.at[1, :, high], up),
     ]
-    combine(2, every)
     attend(0, (2,), sends=((2,),))
+    combine(0, (0, 1))
     product = output(2)
     for copies, cut in zip(far_sum, cuts):
         arrived(copies)
@@ -427,7 +431,6 @@
             send(nsend.at[1, :, low, cut], nrecv.at[0, :, high, cut], down),
             send(nsend.at[1, :, high, cut], nrecv.at[1, :, low, cut], up),
         ]
-    combine(0, (0, 1))
     combine(0, (2,))
     xcols_copy.wait()
     position = index_ref[0]
@@ -504,7 +507,11 @@
         guidance,
     )
     return pl.pallas_call(
-        hand_over, name="hand_over", out_shape=(out, out), in_specs=[vmem, vmem], out_specs=(vmem, vmem)
+        hand_over,
+        name="hand_over",
+        out_shape=(out, out),
+        in_specs=[vmem, vmem],
+        out_specs=(vmem, vmem),
     )(guided, latents_after)
 
 

time: 78.3 us -> 76.3 us (0.974)
  Pallas kernels: 76.2 us -> 74.3 us
    pallas_call x1, Pallas kernels: 74.2 us -> 72.2 us  [per_device(): pl.pallas_call(step_kernel, name='denoising_step', out_shape=(out, out),...]
where the time goes in v4:
time: 76.3 us; the launch traced here: 76.2 us
  Pallas kernels  74.3 us (97%)
  between operations  1.93 us (3%)
    pallas_call x1, Pallas kernels, per_device(): pl.pallas_call(step_kernel, name='denoising_step', out_shape=(out, out),...  72.2 us
    pallas_call x1, Pallas kernels, per_device(): pl.pallas_call(hand_over, name='hand_over', out_shape=(out, out), in_spec...  2.02 us

profile of v4, /device:TPU:1, one launch (start us, length us, event | category | flops | bytes accessed | tf_op | source)
XLA Modules:
  0.0 76.2 jit_solution(2117426580761599664)
XLA Ops:
  1.9 72.2 %denoising_step.1 = (bf16[128,1536]{1,0:T(8,128)(2,1)}, bf16[128,1536]{1,0:T(8,128)(2,1)}) custom-call(bf16[128,3072]{1,0:T(8,128)(2,1)} %x_hbm.1, bf16[3,3072,768]{2,1,0:T(8,128)(2,1)} %bitcast.3, bf16[768,3072]{1,0:T(8,128)(2,1)} %wout_hbm.1, bf16[2,2,256,768]{3,2,1,0:T(8,128)(2,1)} %text_hbm.1, f32[1,128]{1,0:T(1,128)} %bitcast.4, f32[1,128]{1,0:T(1,128)} %bitcast.5, ...), custom_call_target="tpu_custom_call" | custom-call | flops 12000000000 | bytes 15000000 | tf_op jit(solution)/shard_map/denoising_step/pallas_call | solution.py:460
  74.2 2.0 %hand_over.1 = (bf16[128,1536]{1,0:T(8,128)(2,1)}, bf16[128,1536]{1,0:T(8,128)(2,1)}) custom-call(bf16[128,1536]{1,0:T(8,128)(2,1)} %get-tuple-element.4.guided_ref, bf16[128,1536]{1,0:T(8,128)(2,1)} %get-tuple-element.5.next_ref), custom_call_target="tpu_custom_call" | custom-call | tf_op jit(solution)/shard_map/hand_over/pallas_call | solution.py:509

commit v5 on v4

--- a/solution.py
+++ b/solution.py
@@ -68,6 +68,8 @@
     orecv,
     oown,
     lown,
+    kept,
+    keptstat,
     asend,
     abuf,
     dsend,
@@ -265,8 +267,8 @@
 
     back = {}
 
-    def attend(unit, heads, sends):
-        steps = [(head, pair) for head in heads for pair in range(2)]
+    def attend(unit, heads, sends=(), pairs=(0, 1)):
+        steps = [(head, pair) for head in heads for pair in pairs]
         scores_of = {}
 
         def score(head, pair):
@@ -279,6 +281,8 @@
             if n + 1 < len(steps):
                 scores_of[steps[n + 1]] = score(*steps[n + 1])
             scores = scores_of.pop((head, pair))
+            if pairs == (1,):
+                top, total, weighted = keptstat[head, 0:1], keptstat[head, 1:2], kept[head]
             new_top = jnp.max(scores, axis=0, keepdims=True)
             if pair:
                 new_top = jnp.maximum(new_top, top)
@@ -293,6 +297,8 @@
                 part_total = total * shrink + part_total
                 product = weighted * shrink + product
             top, total, weighted = new_top, part_total, product
+            if pairs == (0,):
+                keptstat[head, 0:1], keptstat[head, 1:2], kept[head] = top, total, weighted
             if not pair:
                 continue
             result = weighted / total
@@ -381,18 +387,17 @@
             copy.wait_recv()
 
     every = (0, 1, 2)
+    arrived(far_q[1])
+    attend(1, every, pairs=(0,))
     for unit in range(UNITS):
         arrived(far_kv[unit])
     arrived(far_q[3])
     send_near_q(2)
     attend(3, every, sends=((0, 1), (2,)))
     send_far_q(2)
-    arrived(far_q[1])
-    attend(1, (0, 1), sends=())
+    attend(1, every, sends=(every,), pairs=(1,))
     combine(3, (0, 1))
     combine(3, (2,))
-    attend(1, (2,), sends=())
-    send_back(1, every)
     arrived(far_q[2])
     attend(2, every, sends=(every,))
     for copy in wo_copies:
@@ -478,6 +483,8 @@
             pltpu.VMEM((UNITS, 3, HEADS, HD + STAT, UNIT), BF16),
             pltpu.VMEM((UNITS, HEADS, HD, UNIT), F32),
             pltpu.VMEM((UNITS, 8, UNIT), F32),
+            pltpu.VMEM((HEADS, HD, QUERIES), F32),
+            pltpu.VMEM((HEADS, 8, QUERIES), F32),
             pltpu.VMEM((UNITS, 2, ROWS, OWN), BF16),
             pltpu.VMEM((UNITS, 2, ROWS, 2 * OWN), BF16),
             pltpu.VMEM((2, ROWS, HALF), BF16),

time: 76.3 us -> 76.2 us (level)
  no operation moved by 1% of the time
where the time goes in v5:
time: 76.2 us; the launch traced here: 76.1 us
  Pallas kernels  74.1 us (97%)
  between operations  1.93 us (3%)
    pallas_call x1, Pallas kernels, per_device(): pl.pallas_call(step_kernel, name='denoising_step', out_shape=(out, out),...  72.1 us
    pallas_call x1, Pallas kernels, per_device(): pl.pallas_call(hand_over, name='hand_over', out_shape=(out, out), in_spec...  2.02 us

profile of v5, /device:TPU:1, one launch (start us, length us, event | category | flops | bytes accessed | tf_op | source)
XLA Modules:
  0.0 76.1 jit_solution(7130969012182757576)
XLA Ops:
  1.9 72.1 %denoising_step.1 = (bf16[128,1536]{1,0:T(8,128)(2,1)}, bf16[128,1536]{1,0:T(8,128)(2,1)}) custom-call(bf16[128,3072]{1,0:T(8,128)(2,1)} %x_hbm.1, bf16[3,3072,768]{2,1,0:T(8,128)(2,1)} %bitcast.3, bf16[768,3072]{1,0:T(8,128)(2,1)} %wout_hbm.1, bf16[2,2,256,768]{3,2,1,0:T(8,128)(2,1)} %text_hbm.1, f32[1,128]{1,0:T(1,128)} %bitcast.4, f32[1,128]{1,0:T(1,128)} %bitcast.5, ...), custom_call_target="tpu_custom_call" | custom-call | flops 12000000000 | bytes 15000000 | tf_op jit(solution)/shard_map/denoising_step/pallas_call | solution.py:465
  74.0 2.0 %hand_over.1 = (bf16[128,1536]{1,0:T(8,128)(2,1)}, bf16[128,1536]{1,0:T(8,128)(2,1)}) custom-call(bf16[128,1536]{1,0:T(8,128)(2,1)} %get-tuple-element.4.guided_ref, bf16[128,1536]{1,0:T(8,128)(2,1)} %get-tuple-element.5.next_ref), custom_call_target="tpu_custom_call" | custom-call | tf_op jit(solution)/shard_map/hand_over/pallas_call | solution.py:516
